TPU v7x, 768 devices: a whole 4x8x12 slice. The times are simulated.
768 devices in a mesh: lat: 12 (over z), lon: 64 (over x, y, core).
Axes of the slice: x: 4, y: 8, z: 12, core: 2. Of those that a mesh axis runs over, the one named last changes fastest.
Arguments:
- fields: float32 [768, 1152, 128], P('lat', 'lon'), may hold values from -6 to 6
- cutoff: int32 [768], replicated, may hold values from 2 to 288
- cap_mask: int32 [768], replicated, may hold values from 0 to 1, as said below
- coef_lon: float32 [768, 1152], P('lat', 'lon'), may hold values from 0.02 to 0.16
- coef_lat: float32 [768, 1152], P('lat', 'lon'), may hold values from 0.02 to 0.16
- coef_vert: float32 [768, 1152], P('lat', 'lon'), may hold values from 0.02 to 0.16
Outputs:
- updated: float32 [768, 1152, 128], P('lat', 'lon')
Inputs may be any that keep to these rules, and one draw needn't show every extreme that they name: cap_mask is 1 on the first 96 and the last 96 latitudes, 0 on latitudes 768//4 to 575, and 0 or 1 for each latitude in between.
All inputs are finite; a program needn't handle non-finite values.
Results may differ from a plain program's by a relative error of at most 0.0003.
Values sent between devices are 32-bit elements; how exact they have to be, the bound alone decides.
No kernel may reach another device: no remote copies, remote signals or barrier semaphores. Data moves between devices by JAX's collectives and lax.ppermute only.
A program may use at most 64 MiB of HBM per device.

v0:
```python
import functools

import jax
import jax.numpy as jnp
import ml_dtypes
import numpy as np
from jax import lax
from jax.experimental import pallas as pl
from jax.experimental.pallas import tpu as pltpu
from jax.sharding import PartitionSpec as P

LEV = 16
WAVES = 288


def split_table(table):
    high = table.astype(ml_dtypes.bfloat16)
    low = (table - high.astype(np.float64)).astype(ml_dtypes.bfloat16)
    return np.concatenate([high, low], axis=0)


def tables(full, cols):
    half = full // 2
    sectors = half // cols
    place = (np.arange(cols)[:, None] + cols * np.arange(sectors)[None, :]).reshape(-1)
    made = []
    for parity in (0, 1):
        wave = np.arange(parity, WAVES, 2)
        angle = (wave[:, None] * place[None, :] % full) * (2.0 * np.pi / full)
        made.append(np.concatenate([np.cos(angle), np.sin(angle)], axis=0))
    return [split_table(m) for m in made] + [split_table(m.T) for m in made]


def pack_kernel(x_ref, out_ref):
    cols, rows, _ = x_ref.shape
    for j in range(cols):
        out_ref[pl.ds(j, rows, stride=cols), :] = x_ref[j]


def halves(values):
    high = values.astype(jnp.bfloat16)
    low = (values - high.astype(jnp.float32)).astype(jnp.bfloat16)
    return high, low


def product(table_ref, data):
    both = jnp.dot(table_ref[...], data, preferred_element_type=jnp.float32)
    rows = both.shape[0] // 2
    depth = both.shape[1] // 2
    return (both[:rows, :depth] + both[:rows, depth:]) + (both[rows:, :depth] + both[rows:, depth:])


def filter_kernel(cols, peers, cut_ref, cap_ref, x_ref, fe_ref, fo_ref, be_ref, bo_ref, out_ref, even, odd):
    depth = x_ref.shape[1]
    full = cols * peers
    half = peers // 2
    wide = cols + 2
    row = lax.axis_index("lat") * peers + lax.axis_index("lon")
    cut = cut_ref[row]
    cap = cap_ref[row]

    def emit(j, values):
        out_ref[pl.ds(1 + j, peers, stride=wide), :] = values
        if j == cols - 1:
            out_ref[pl.ds(0, peers, stride=wide), :] = pltpu.roll(values, 1, 0)
        if j == 0:
            out_ref[pl.ds(wide - 1, peers, stride=wide), :] = pltpu.roll(values, peers - 1, 0)

    @pl.when(cap != 1)
    def _():
        for j in range(cols):
            emit(j, x_ref[pl.ds(j, peers, stride=cols), :])

    @pl.when(cap == 1)
    def _():
        for j in range(cols):
            values = x_ref[pl.ds(j, peers, stride=cols), :]
            for ref, folded in ((even, values[:half] + values[half:]), (odd, values[:half] - values[half:])):
                high, low = halves(folded)
                ref[pl.ds(j * half, half), 0:depth] = high
                ref[pl.ds(j * half, half), depth : 2 * depth] = low
        back = []
        for parity, ref, forth_ref, back_ref in ((0, even, fe_ref, be_ref), (1, odd, fo_ref, bo_ref)):
            spectrum = product(forth_ref, ref[...])
            index = lax.broadcasted_iota(jnp.int32, spectrum.shape, 0)
            count = WAVES // 2
            wave = 2 * jnp.where(index < count, index, index - count) + parity
            weight = jnp.where(wave == 0, 1.0 / full, 2.0 / full)
            spectrum = jnp.where(wave < cut, spectrum * weight, 0.0)
            back.append(product(back_ref, jnp.concatenate(halves(spectrum), axis=1)))
        for j in range(cols):
            near = back[0][j * half : (j + 1) * half]
            far = back[1][j * half : (j + 1) * half]
            emit(j, jnp.concatenate([near + far, near - far], axis=0))


def stencil_kernel(cols, rows, n_lat, g_ref, north_ref, south_ref, far_ref, cl_ref, ct_ref, cv_ref, out_ref):
    wide = cols + 2
    depth = g_ref.shape[1]
    lat = lax.axis_index("lat")
    lane = lax.broadcasted_iota(jnp.int32, (rows, depth), 1)
    line = lax.broadcasted_iota(jnp.int32, (rows, depth), 0)
    top = lane % LEV == LEV - 1
    bottom = lane % LEV == 0
    sign = jnp.where(lax.broadcasted_iota(jnp.int32, (cols, depth), 1) < 2 * LEV, -1.0, 1.0)
    north = jnp.where(lat == 0, sign * far_ref[0], north_ref[...])
    south = jnp.where(lat == n_lat - 1, sign * far_ref[1], south_ref[...])
    coefs = [jnp.transpose(ref[...]) for ref in (cl_ref, ct_ref, cv_ref)]
    line_of = [g_ref[pl.ds(i, rows, stride=wide), :] for i in range(2)]
    for j in range(cols):
        line_of.append(g_ref[pl.ds(j + 2, rows, stride=wide), :])
        west, here, east = line_of[j : j + 3]
        up = jnp.where(line == 0, north[j : j + 1], pltpu.roll(here, 1, 0))
        down = jnp.where(line == rows - 1, south[j : j + 1], pltpu.roll(here, rows - 1, 0))
        above = jnp.where(top, 0.0, pltpu.roll(here, depth - 1, 1))
        below = jnp.where(bottom, 0.0, pltpu.roll(here, 1, 1))
        twice = 2.0 * here
        out_ref[j] = (
            here
            + coefs[0][:, j : j + 1] * (east + west - twice)
            + coefs[1][:, j : j + 1] * (up + down - twice)
            + coefs[2][:, j : j + 1] * (above + below - twice)
        )


def per_device(fields, cutoff, cap_mask, coef_lon, coef_lat, coef_vert):
    rows, cols, depth = fields.shape
    peers = lax.axis_size("lon")
    n_lat = lax.axis_size("lat")
    vmem = pl.BlockSpec(memory_space=pltpu.VMEM)
    smem = pl.BlockSpec(memory_space=pltpu.SMEM)
    wide = cols + 2

    packed = pl.pallas_call(
        pack_kernel,
        out_shape=jax.ShapeDtypeStruct((rows * cols, depth), jnp.float32),
        in_specs=[vmem],
        out_specs=vmem,
        name="pack",
    )(jnp.transpose(fields, (1, 0, 2)))
    block = lax.all_to_all(packed.reshape(peers, cols, 1, depth), "lon", 0, 0, tiled=True)
    forth_even, forth_odd, back_even, back_odd = tables(cols * peers, cols)
    half = cols * peers // 2
    filtered = pl.pallas_call(
        functools.partial(filter_kernel, cols, peers),
        out_shape=jax.ShapeDtypeStruct((peers * wide, depth), jnp.float32),
        in_specs=[smem, smem] + [vmem] * 5,
        out_specs=vmem,
        scratch_shapes=[pltpu.VMEM((half, 2 * depth), jnp.bfloat16)] * 2,
        compiler_params=pltpu.CompilerParams(vmem_limit_bytes=24 * 1024 * 1024),
        name="filter",
    )(
        cutoff,
        cap_mask,
        block.reshape(peers * cols, depth),
        jnp.asarray(forth_even),
        jnp.asarray(forth_odd),
        jnp.asarray(back_even),
        jnp.asarray(back_odd),
    )
    returned = lax.all_to_all(filtered.reshape(peers, wide, 1, depth), "lon", 0, 0, tiled=True)
    head = returned[0, 1:-1, 0]
    tail = returned[-1, 1:-1, 0]
    ring = [(i, (i + 1) % n_lat) for i in range(n_lat)]
    north = lax.ppermute(tail, "lat", ring)
    south = lax.ppermute(head, "lat", [(b, a) for a, b in ring])
    far = lax.ppermute(jnp.stack([head, tail]), "lon", [(i, (i + peers // 2) % peers) for i in range(peers)])
    out = pl.pallas_call(
        functools.partial(stencil_kernel, cols, rows, n_lat),
        out_shape=jax.ShapeDtypeStruct((cols, rows, depth), jnp.float32),
        in_specs=[vmem] * 7,
        out_specs=vmem,
        name="stencil",
    )(
        returned.reshape(rows * wide, depth),
        north,
        south,
        far,
        jnp.transpose(coef_lon),
        jnp.transpose(coef_lat),
        jnp.transpose(coef_vert),
    )
    return jnp.transpose(out, (1, 0, 2))


def solution(mesh):
    return jax.shard_map(
        per_device,
        mesh=mesh,
        in_specs=(
            P("lat", "lon", None),
            P(),
            P(),
            P("lat", "lon"),
            P("lat", "lon"),
            P("lat", "lon"),
        ),
        out_specs=P("lat", "lon", None),
        check_vma=False,
    )
```

profile of v0, /device:TPU:1, one launch (start us, length us, event | category | flops | bytes accessed | tf_op | source)
XLA Modules:
  0.0 89.1 jit_solution(8848557340229566351)
XLA Ops:
  0.0 0.0 copy-start.1
  0.0 2.0 %pack.1 = f32[1152,128]{1,0:T(8,128)} custom-call(f32[18,64,128]{2,1,0:T(8,128)} %bitcast.23), custom_call_target="tpu_custom_call" | custom-call | tf_op jit(solution)/shard_map/pack/pallas_call | solution.py:134
  2.0 0.0 copy-start
  2.0 0.0 copy-start.4
  2.0 0.0 copy-start.5
  2.0 33.6 %all_to_all.10 = f32[64,18,1,128]{3,2,1,0:T(1,128)S(1)} all-to-all(f32[64,18,1,128]{3,2,1,0:T(1,128)} %bitcast.22), channel_id=1, replica_groups=mesh['lat'=12,'lon'=64] {'lon'}, dimensions={0} | all-to-all | bytes 1179648 | tf_op jit(solution)/shard_map/all_to_all | solution.py:141
  35.6 0.0 copy-done.1
  35.6 0.0 copy-done
  35.6 0.0 copy-done.4
  35.6 0.0 copy-done.5
  35.6 0.0 copy-start.2
  35.6 1.1 %copy-done.2 = bf16[576,576]{1,0:T(8,128)(2,1)S(1)} copy-done((bf16[576,576]{1,0:T(8,128)(2,1)S(1)}, bf16[576,576]{1,0:T(8,128)(2,1)}, u32[]{:S(2)}) %copy-start.2) | copy-done | bytes 663576
  36.7 0.0 copy-start.3
  36.7 1.1 %copy-done.3 = bf16[576,576]{1,0:T(8,128)(2,1)S(1)} copy-done((bf16[576,576]{1,0:T(8,128)(2,1)S(1)}, bf16[576,576]{1,0:T(8,128)(2,1)}, u32[]{:S(2)}) %copy-start.3) | copy-done | bytes 663576
  37.8 2.8 %filter.1 = f32[1280,128]{1,0:T(8,128)S(1)} custom-call(s32[768]{0:T(1024)S(1)} %copy-done.4, s32[768]{0:T(1024)S(1)} %copy-done.5, f32[1152,128]{1,0:T(8,128)S(1)} %bitcast.20, bf16[576,576]{1,0:T(8,128)(2,1)S(1)} %copy-done.3, bf16[576,576]{1,0:T(8,128)(2,1)S(1)} %copy-done.2, bf16[1152,288]{1,0:T(8,128)(2,1)S(1)} %copy-done.1, bf16[1152,288]{1,0:T(8,128)(2,1)S(1)} %copy-done), custom_call_target="tpu_custom_call" | custom-call | tf_op jit(solution)/shard_map/filter/pallas_call | solution.py:144
  40.6 26.3 %all_to_all.11 = f32[64,20,1,128]{3,2,1,0:T(1,128)S(1)} all-to-all(f32[64,20,1,128]{3,2,1,0:T(1,128)S(1)} %bitcast.19), channel_id=1, replica_groups=mesh['lat'=12,'lon'=64] {'lon'}, dimensions={0} | all-to-all | bytes 1310720 | tf_op jit(solution)/shard_map/all_to_all | solution.py:161
  66.9 0.0 copy-start.6
  66.9 4.7 %collective-permute-start.2 = (f32[2,18,128]{2,1,0:T(8,128)S(1)}, f32[2,18,128]{2,1,0:T(8,128)S(1)}, u32[]{:S(2)}, u32[]{:S(2)}) collective-permute-start(f32[2,18,128]{2,1,0:T(8,128)S(1)} %pad_maximum_fusion), channel_id=1, source_target_pairs={{0,32},{1,33},{2,34},{3,35},{4,36},{5,37},{6,38},{7,39},{8,40},{9,... | collective-permute-start | bytes 55304 | tf_op jit(solution)/shard_map/ppermute | solution.py:167
  71.7 1.9 %collective-permute-start = (f32[18,128]{1,0:T(8,128)S(1)}, f32[18,128]{1,0:T(8,128)S(1)}, u32[]{:S(2)}, u32[]{:S(2)}) collective-permute-start(f32[18,128]{1,0:T(8,128)S(1)} %bitcast.27), channel_id=1, source_target_pairs={{0,64},{64,128},{128,192},{192,256},{256,320},{320,384},{384,448},... | collective-permute-start | bytes 27656 | tf_op jit(solution)/shard_map/ppermute | solution.py:165
  73.6 11.2 %collective-permute-start.1 = (f32[18,128]{1,0:T(8,128)S(1)}, f32[18,128]{1,0:T(8,128)S(1)}, u32[]{:S(2)}, u32[]{:S(2)}) collective-permute-start(f32[18,128]{1,0:T(8,128)S(1)} %bitcast.25), channel_id=1, source_target_pairs={{64,0},{128,64},{192,128},{256,192},{320,256},{384,320},{448,384},... | collective-permute-start | bytes 27656 | tf_op jit(solution)/shard_map/ppermute | solution.py:166
  84.8 0.0 collective-permute-done.north_ref
  84.8 0.0 copy-start.8
  84.8 0.8 collective-permute-done.1.south_ref
  85.6 0.0 copy-start.9
  85.6 0.0 collective-permute-done.2.far_ref
  85.6 0.0 copy-start.7
  85.6 0.0 copy-done.6
  85.6 0.0 copy-done.8
  85.6 0.6 copy-done.9
  86.2 0.0 copy-done.7
  86.2 2.9 %stencil.1 = f32[18,64,128]{2,1,0:T(8,128)} custom-call(f32[1280,128]{1,0:T(8,128)} %bitcast.21, f32[18,128]{1,0:T(8,128)} %copy-done.8, f32[18,128]{1,0:T(8,128)} %copy-done.9, f32[2,18,128]{2,1,0:T(8,128)} %copy-done.7, f32[18,64]{1,0:T(8,128)} %bitcast.28, f32[18,64]{1,0:T(8,128)} %bitcast.29, f32[18,64]{1,0:T(8,128)} %bitcast.30), custom_call_target="tpu_custom_call" | custom-call | tf_op jit(solution)/shard_map/stencil/pallas_call | solution.py:168
  (4 shorter events, 0.0 us)
Async XLA Ops:
  0.0 35.6 %copy-start.1 = (bf16[1152,288]{1,0:T(8,128)(2,1)S(1)}, bf16[1152,288]{1,0:T(8,128)(2,1)}, u32[]{:S(2)}) copy-start(bf16[1152,288]{1,0:T(8,128)(2,1)} %constant.10.clone.be_ref) | copy-start | bytes 1990660
  2.0 33.6 %copy-start = (bf16[1152,288]{1,0:T(8,128)(2,1)S(1)}, bf16[1152,288]{1,0:T(8,128)(2,1)}, u32[]{:S(2)}) copy-start(bf16[1152,288]{1,0:T(8,128)(2,1)} %constant.11.clone.bo_ref) | copy-start | bytes 1990660
  2.0 33.6 %copy-start.4 = (s32[768]{0:T(1024)S(1)}, s32[768]{0:T(1024)}, u32[]{:S(2)}) copy-start(s32[768]{0:T(1024)} %cut_ref.1) | copy-start | bytes 9220
  2.0 33.6 %copy-start.5 = (s32[768]{0:T(1024)S(1)}, s32[768]{0:T(1024)}, u32[]{:S(2)}) copy-start(s32[768]{0:T(1024)} %cap_ref.1) | copy-start | bytes 9220
  35.6 1.1 %copy-start.2 = (bf16[576,576]{1,0:T(8,128)(2,1)S(1)}, bf16[576,576]{1,0:T(8,128)(2,1)}, u32[]{:S(2)}) copy-start(bf16[576,576]{1,0:T(8,128)(2,1)} %constant.9.clone.fo_ref) | copy-start | bytes 1990660
  36.7 1.1 %copy-start.3 = (bf16[576,576]{1,0:T(8,128)(2,1)S(1)}, bf16[576,576]{1,0:T(8,128)(2,1)}, u32[]{:S(2)}) copy-start(bf16[576,576]{1,0:T(8,128)(2,1)} %constant.8.clone.fe_ref) | copy-start | bytes 1990660
  66.9 18.7 %copy-start.6 = (f32[64,20,1,128]{3,2,1,0:T(1,128)}, f32[64,20,1,128]{3,2,1,0:T(1,128)S(1)}, u32[]{:S(2)}) copy-start(f32[64,20,1,128]{3,2,1,0:T(1,128)S(1)} %all_to_all.11) | copy-start | bytes 1966084
  66.9 18.7 %collective-permute-start.2 = (f32[2,18,128]{2,1,0:T(8,128)S(1)}, f32[2,18,128]{2,1,0:T(8,128)S(1)}, u32[]{:S(2)}, u32[]{:S(2)}) collective-permute-start(f32[2,18,128]{2,1,0:T(8,128)S(1)} %pad_maximum_fusion), channel_id=1, source_target_pairs={{0,32},{1,33},{2,34},{3,35},{4,36},{5,37},{6,38},{7,39},{8,40},{9,... | collective-permute-start | bytes 55304 | tf_op jit(solution)/shard_map/ppermute | solution.py:167
  71.7 13.1 %collective-permute-start = (f32[18,128]{1,0:T(8,128)S(1)}, f32[18,128]{1,0:T(8,128)S(1)}, u32[]{:S(2)}, u32[]{:S(2)}) collective-permute-start(f32[18,128]{1,0:T(8,128)S(1)} %bitcast.27), channel_id=1, source_target_pairs={{0,64},{64,128},{128,192},{192,256},{256,320},{320,384},{384,448},... | collective-permute-start | bytes 27656 | tf_op jit(solution)/shard_map/ppermute | solution.py:165
  73.6 12.0 %collective-permute-start.1 = (f32[18,128]{1,0:T(8,128)S(1)}, f32[18,128]{1,0:T(8,128)S(1)}, u32[]{:S(2)}, u32[]{:S(2)}) collective-permute-start(f32[18,128]{1,0:T(8,128)S(1)} %bitcast.25), channel_id=1, source_target_pairs={{64,0},{128,64},{192,128},{256,192},{320,256},{384,320},{448,384},... | collective-permute-start | bytes 27656 | tf_op jit(solution)/shard_map/ppermute | solution.py:166
  84.8 0.8 copy-start.8
  85.6 0.6 copy-start.9
  85.6 0.6 copy-start.7
where the time goes:
time: 89.6 us; the launch traced here: 89.1 us
  blocking collectives  59.8 us (67%)
  starting transfers between devices  17.8 us (20%)
  Pallas kernels  7.73 us (9%)
  local copies, waits for them, and re-layouts  2.85 us (3%)
    all_to_all x1, blocking collectives, per_device(): lax.all_to_all(packed.reshape(peers, cols, 1, depth), 'lon', 0, 0, tiled=...  33.6 us
    all_to_all x1, blocking collectives, per_device(): lax.all_to_all(filtered.reshape(peers, wide, 1, depth), 'lon', 0, 0, tile...  26.3 us
    ppermute x1, starting transfers between devices, per_device(): south = lax.ppermute(head, 'lat', [(b, a) for a, b in ring])  11.2 us
    ppermute x1, starting transfers between devices, per_device(): lax.ppermute(jnp.stack([head, tail]), 'lon', [(i, (i + peers // 2) % peer...  4.75 us
    pallas_call x1, Pallas kernels, per_device(): pl.pallas_call(functools.partial(stencil_kernel, cols, rows, n_lat), out_...  2.93 us
    unnamed x22, local copies, waits for them, and re-layouts  2.84 us
    pallas_call x1, Pallas kernels, per_device(): pl.pallas_call(functools.partial(filter_kernel, cols, peers), out_shape=j...  2.81 us
    pallas_call x1, Pallas kernels, per_device(): pl.pallas_call(pack_kernel, out_shape=jax.ShapeDtypeStruct((rows * cols,...  2 us
  transfers between devices with their start and end apart: 3, of which 1 were waited for; matrix products, arithmetic and copies ran while one was open for 0% of the time, Pallas kernels for 0%

commit v1 on v0

--- a/solution.py
+++ b/solution.py
@@ -28,13 +28,24 @@
         wave = np.arange(parity, WAVES, 2)
         angle = (wave[:, None] * place[None, :] % full) * (2.0 * np.pi / full)
         made.append(np.concatenate([np.cos(angle), np.sin(angle)], axis=0))
-    return [split_table(m) for m in made] + [split_table(m.T) for m in made]
-
-
-def pack_kernel(x_ref, out_ref):
+    forth = np.concatenate([split_table(m) for m in made], axis=0)
+    back = np.concatenate([split_table(m.T) for m in made], axis=0)
+    return forth, back
+
+
+def pack_kernel(x_ref, out_ref, held, sems):
     cols, rows, _ = x_ref.shape
-    for j in range(cols):
-        out_ref[pl.ds(j, rows, stride=cols), :] = x_ref[j]
+    parts = sems.shape[0]
+    size = cols // parts
+    copies = []
+    for i in range(parts):
+        part = pl.ds(i * size, size)
+        copies.append(pltpu.make_async_copy(x_ref.at[part], held.at[part], sems.at[i]))
+        copies[-1].start()
+    for i in range(parts):
+        copies[i].wait()
+        for j in range(i * size, (i + 1) * size):
+            out_ref[pl.ds(j, rows, stride=cols), :] = held[j]
 
 
 def halves(values):
@@ -43,14 +54,14 @@
     return high, low
 
 
-def product(table_ref, data):
-    both = jnp.dot(table_ref[...], data, preferred_element_type=jnp.float32)
+def product(table, data):
+    both = jnp.dot(table, data, preferred_element_type=jnp.float32)
     rows = both.shape[0] // 2
     depth = both.shape[1] // 2
     return (both[:rows, :depth] + both[:rows, depth:]) + (both[rows:, :depth] + both[rows:, depth:])
 
 
-def filter_kernel(cols, peers, cut_ref, cap_ref, x_ref, fe_ref, fo_ref, be_ref, bo_ref, out_ref, even, odd):
+def filter_kernel(cols, peers, cut_ref, cap_ref, x_ref, forth_ref, back_ref, out_ref, even, odd):
     depth = x_ref.shape[1]
     full = cols * peers
     half = peers // 2
@@ -80,47 +91,61 @@
                 ref[pl.ds(j * half, half), 0:depth] = high
                 ref[pl.ds(j * half, half), depth : 2 * depth] = low
         back = []
-        for parity, ref, forth_ref, back_ref in ((0, even, fe_ref, be_ref), (1, odd, fo_ref, bo_ref)):
-            spectrum = product(forth_ref, ref[...])
+        for parity, ref in ((0, even), (1, odd)):
+            spectrum = product(forth_ref[pl.ds(parity * 2 * WAVES, 2 * WAVES), :], ref[...])
             index = lax.broadcasted_iota(jnp.int32, spectrum.shape, 0)
             count = WAVES // 2
             wave = 2 * jnp.where(index < count, index, index - count) + parity
             weight = jnp.where(wave == 0, 1.0 / full, 2.0 / full)
             spectrum = jnp.where(wave < cut, spectrum * weight, 0.0)
-            back.append(product(back_ref, jnp.concatenate(halves(spectrum), axis=1)))
+            table = back_ref[pl.ds(parity * full, full), :]
+            back.append(product(table, jnp.concatenate(halves(spectrum), axis=1)))
         for j in range(cols):
             near = back[0][j * half : (j + 1) * half]
             far = back[1][j * half : (j + 1) * half]
             emit(j, jnp.concatenate([near + far, near - far], axis=0))
 
 
-def stencil_kernel(cols, rows, n_lat, g_ref, north_ref, south_ref, far_ref, cl_ref, ct_ref, cv_ref, out_ref):
+def stencil_kernel(cols, rows, n_lat, g_ref, first_ref, second_ref, cl_ref, ct_ref, cv_ref, out_ref, made, sems):
     wide = cols + 2
     depth = g_ref.shape[1]
+    parts = sems.shape[0]
+    size = cols // parts
     lat = lax.axis_index("lat")
+    odd = lat % 2 == 1
     lane = lax.broadcasted_iota(jnp.int32, (rows, depth), 1)
     line = lax.broadcasted_iota(jnp.int32, (rows, depth), 0)
     top = lane % LEV == LEV - 1
     bottom = lane % LEV == 0
-    sign = jnp.where(lax.broadcasted_iota(jnp.int32, (cols, depth), 1) < 2 * LEV, -1.0, 1.0)
-    north = jnp.where(lat == 0, sign * far_ref[0], north_ref[...])
-    south = jnp.where(lat == n_lat - 1, sign * far_ref[1], south_ref[...])
+    flip = jnp.where(lax.broadcasted_iota(jnp.int32, (1, depth), 1) < 2 * LEV, -1.0, 1.0)
+    north_sign = jnp.where(lat == 0, flip, 1.0)
+    south_sign = jnp.where(lat == n_lat - 1, flip, 1.0)
     coefs = [jnp.transpose(ref[...]) for ref in (cl_ref, ct_ref, cv_ref)]
     line_of = [g_ref[pl.ds(i, rows, stride=wide), :] for i in range(2)]
+    copies = []
     for j in range(cols):
         line_of.append(g_ref[pl.ds(j + 2, rows, stride=wide), :])
         west, here, east = line_of[j : j + 3]
-        up = jnp.where(line == 0, north[j : j + 1], pltpu.roll(here, 1, 0))
-        down = jnp.where(line == rows - 1, south[j : j + 1], pltpu.roll(here, rows - 1, 0))
+        first, second = first_ref[j + 1], second_ref[j + 1]
+        north = north_sign * jnp.where(odd, second, first)
+        south = south_sign * jnp.where(odd, first, second)
+        up = jnp.where(line == 0, north, pltpu.roll(here, 1, 0))
+        down = jnp.where(line == rows - 1, south, pltpu.roll(here, rows - 1, 0))
         above = jnp.where(top, 0.0, pltpu.roll(here, depth - 1, 1))
         below = jnp.where(bottom, 0.0, pltpu.roll(here, 1, 1))
         twice = 2.0 * here
-        out_ref[j] = (
+        made[j] = (
             here
             + coefs[0][:, j : j + 1] * (east + west - twice)
             + coefs[1][:, j : j + 1] * (up + down - twice)
             + coefs[2][:, j : j + 1] * (above + below - twice)
         )
+        if (j + 1) % size == 0:
+            part = pl.ds(j + 1 - size, size)
+            copies.append(pltpu.make_async_copy(made.at[part], out_ref.at[part], sems.at[j // size]))
+            copies[-1].start()
+    for copy in copies:
+        copy.wait()
 
 
 def per_device(fields, cutoff, cap_mask, coef_lon, coef_lat, coef_vert):
@@ -134,17 +159,18 @@
     packed = pl.pallas_call(
         pack_kernel,
         out_shape=jax.ShapeDtypeStruct((rows * cols, depth), jnp.float32),
-        in_specs=[vmem],
+        in_specs=[pl.BlockSpec(memory_space=pl.ANY)],
         out_specs=vmem,
+        scratch_shapes=[pltpu.VMEM((cols, rows, depth), jnp.float32), pltpu.SemaphoreType.DMA((6,))],
         name="pack",
     )(jnp.transpose(fields, (1, 0, 2)))
     block = lax.all_to_all(packed.reshape(peers, cols, 1, depth), "lon", 0, 0, tiled=True)
-    forth_even, forth_odd, back_even, back_odd = tables(cols * peers, cols)
+    forth, back = tables(cols * peers, cols)
     half = cols * peers // 2
     filtered = pl.pallas_call(
         functools.partial(filter_kernel, cols, peers),
         out_shape=jax.ShapeDtypeStruct((peers * wide, depth), jnp.float32),
-        in_specs=[smem, smem] + [vmem] * 5,
+        in_specs=[smem, smem] + [vmem] * 3,
         out_specs=vmem,
         scratch_shapes=[pltpu.VMEM((half, 2 * depth), jnp.bfloat16)] * 2,
         compiler_params=pltpu.CompilerParams(vmem_limit_bytes=24 * 1024 * 1024),
@@ -153,29 +179,33 @@
         cutoff,
         cap_mask,
         block.reshape(peers * cols, depth),
-        jnp.asarray(forth_even),
-        jnp.asarray(forth_odd),
-        jnp.asarray(back_even),
-        jnp.asarray(back_odd),
+        jnp.asarray(forth),
+        jnp.asarray(back),
     )
     returned = lax.all_to_all(filtered.reshape(peers, wide, 1, depth), "lon", 0, 0, tiled=True)
-    head = returned[0, 1:-1, 0]
-    tail = returned[-1, 1:-1, 0]
-    ring = [(i, (i + 1) % n_lat) for i in range(n_lat)]
-    north = lax.ppermute(tail, "lat", ring)
-    south = lax.ppermute(head, "lat", [(b, a) for a, b in ring])
-    far = lax.ppermute(jnp.stack([head, tail]), "lon", [(i, (i + peers // 2) % peers) for i in range(peers)])
+    odd = lax.axis_index("lat") % 2 == 1
+    head, tail = returned[0], returned[-1]
+    first, second = [], []
+    for lat in range(n_lat):
+        for lon in range(peers):
+            here = lat * peers + lon
+            pair = lat + 1 if lat % 2 else lat - 1
+            inside = 0 <= pair < n_lat
+            first.append((here, pair * peers + lon if inside else lat * peers + (lon + peers // 2) % peers))
+            second.append((here, (lat ^ 1) * peers + lon))
+    first = lax.ppermute(jnp.where(odd, tail, head), ("lat", "lon"), first)
+    second = lax.ppermute(jnp.where(odd, head, tail), ("lat", "lon"), second)
     out = pl.pallas_call(
         functools.partial(stencil_kernel, cols, rows, n_lat),
         out_shape=jax.ShapeDtypeStruct((cols, rows, depth), jnp.float32),
-        in_specs=[vmem] * 7,
-        out_specs=vmem,
+        in_specs=[vmem] * 6,
+        out_specs=pl.BlockSpec(memory_space=pl.ANY),
+        scratch_shapes=[pltpu.VMEM((cols, rows, depth), jnp.float32), pltpu.SemaphoreType.DMA((6,))],
         name="stencil",
     )(
         returned.reshape(rows * wide, depth),
-        north,
-        south,
-        far,
+        first,
+        second,
         jnp.transpose(coef_lon),
         jnp.transpose(coef_lat),
         jnp.transpose(coef_vert),

time: 89.6 us -> 80.1 us (0.89)
  blocking collectives: 59.8 us -> 33.4 us
  waiting for transfers between devices: 0.79 us -> 22.6 us
  starting transfers between devices: 17.8 us -> 13 us
    all_to_all x1 -> x0, blocking collectives: 26.3 us -> none  [per_device(): lax.all_to_all(filtered.reshape(peers, wide, 1, depth), 'lon', 0, 0, tile...]
    all_to_all x0 -> x1, waiting for transfers between devices: none -> 20.1 us  [per_device(): lax.all_to_all(filtered.reshape(peers, wide, 1, depth), 'lon', 0, 0, tile...]
    ppermute x3 -> x2, starting transfers between devices: 17.8 us -> 6.67 us  [the longest x1 4.75 us: per_device(): first = lax.ppermute(jnp.where(odd, tail, head), ('lat', 'lon'), first)]
    all_to_all x0 -> x1, starting transfers between devices: none -> 6.34 us  [per_device(): lax.all_to_all(filtered.reshape(peers, wide, 1, depth), 'lon', 0, 0, tile...]
    ppermute x3 -> x2, waiting for transfers between devices: 0.79 us -> 2.47 us  [the longest x1 2.47 us: per_device(): second = lax.ppermute(jnp.where(odd, head, tail), ('lat', 'lon'), second)]
    unnamed x22 -> x14, local copies, waits for them, and re-layouts: 2.84 us -> 1.98 us
  transfers between devices with their start and end apart: 3 -> 3, of which waited for: 1 -> 2; matrix products, arithmetic and copies ran while one was open for 0% -> 0% of each run, Pallas kernels for 0% -> 0%
where the time goes in v1:
time: 80.1 us; the launch traced here: 79.7 us
  blocking collectives  33.4 us (42%)
  waiting for transfers between devices  22.6 us (28%)
  starting transfers between devices  13 us (16%)
  Pallas kernels  8.57 us (11%)
  local copies, waits for them, and re-layouts  1.98 us (2%)
    all_to_all x1, blocking collectives, per_device(): lax.all_to_all(packed.reshape(peers, cols, 1, depth), 'lon', 0, 0, tiled=...  33.4 us
    all_to_all x1, waiting for transfers between devices, per_device(): lax.all_to_all(filtered.reshape(peers, wide, 1, depth), 'lon', 0, 0, tile...  20.1 us
    all_to_all x1, starting transfers between devices, per_device(): lax.all_to_all(filtered.reshape(peers, wide, 1, depth), 'lon', 0, 0, tile...  6.34 us
    ppermute x1, starting transfers between devices, per_device(): first = lax.ppermute(jnp.where(odd, tail, head), ('lat', 'lon'), first)  4.75 us
    pallas_call x1, Pallas kernels, per_device(): pl.pallas_call(functools.partial(filter_kernel, cols, peers), out_shape=j...  3.65 us
    pallas_call x1, Pallas kernels, per_device(): pl.pallas_call(functools.partial(stencil_kernel, cols, rows, n_lat), out_...  2.78 us
    ppermute x1, waiting for transfers between devices, per_device(): second = lax.ppermute(jnp.where(odd, head, tail), ('lat', 'lon'), second)  2.47 us
    pallas_call x1, Pallas kernels, per_device(): pl.pallas_call(pack_kernel, out_shape=jax.ShapeDtypeStruct((rows * cols,...  2.13 us
  transfers between devices with their start and end apart: 3, of which 2 were waited for; matrix products, arithmetic and copies ran while one was open for 0% of the time, Pallas kernels for 0%

profile of v1, /device:TPU:1, one launch (start us, length us, event | category | flops | bytes accessed | tf_op | source)
XLA Modules:
  0.0 79.7 jit_solution(996182680927151253)
XLA Ops:
  0.0 0.0 copy-start
  0.0 0.0 copy-start.2
  0.0 0.0 copy-start.3
  0.0 2.1 %pack.1 = f32[1152,128]{1,0:T(8,128)} custom-call(f32[18,64,128]{2,1,0:T(8,128)} %bitcast.16), custom_call_target="tpu_custom_call" | custom-call | tf_op jit(solution)/shard_map/pack/pallas_call | solution.py:159
  2.1 33.4 %all_to_all.10 = f32[64,18,1,128]{3,2,1,0:T(1,128)S(1)} all-to-all(f32[64,18,1,128]{3,2,1,0:T(1,128)} %bitcast.15), channel_id=1, replica_groups=mesh['lat'=12,'lon'=64] {'lon'}, dimensions={0} | all-to-all | bytes 1179648 | tf_op jit(solution)/shard_map/all_to_all | solution.py:167
  35.6 0.0 copy-done
  35.6 0.0 copy-done.2
  35.6 0.0 copy-done.3
  35.6 0.0 copy-start.1
  35.6 1.4 %copy-done.1 = bf16[1152,576]{1,0:T(8,128)(2,1)S(1)} copy-done((bf16[1152,576]{1,0:T(8,128)(2,1)S(1)}, bf16[1152,576]{1,0:T(8,128)(2,1)}, u32[]{:S(2)}) %copy-start.1) | copy-done | bytes 1327128
  37.0 3.7 %filter.1 = f32[1280,128]{1,0:T(8,128)} custom-call(s32[768]{0:T(1024)S(1)} %copy-done.2, s32[768]{0:T(1024)S(1)} %copy-done.3, f32[1152,128]{1,0:T(8,128)S(1)} %bitcast.13, bf16[1152,576]{1,0:T(8,128)(2,1)S(1)} %copy-done.1, bf16[2304,288]{1,0:T(8,128)(2,1)S(1)} %copy-done), custom_call_target="tpu_custom_call" | custom-call | tf_op jit(solution)/shard_map/filter/pallas_call | solution.py:170
  40.6 6.3 %all-to-all-start.1 = ((f32[64,20,1,128]{3,2,1,0:T(1,128)}), f32[64,20,1,128]{3,2,1,0:T(1,128)S(1)}, u32[]{:S(2)}, u32[]{:S(2)}) async-start(f32[64,20,1,128]{3,2,1,0:T(1,128)} %bitcast.3), calls=%async_computation.1 | async-start | bytes 1310720 | tf_op jit(solution)/shard_map/all_to_all | solution.py:185
  47.0 20.1 %all-to-all-done.1 = f32[64,20,1,128]{3,2,1,0:T(1,128)S(1)} async-done(((f32[64,20,1,128]{3,2,1,0:T(1,128)}), f32[64,20,1,128]{3,2,1,0:T(1,128)S(1)}, u32[]{:S(2)}, u32[]{:S(2)}) %all-to-all-start.1) | async-done | bytes 655392 | tf_op jit(solution)/shard_map/all_to_all | solution.py:185
  67.1 0.0 copy-start.4
  67.1 4.7 %collective-permute-start = (f32[20,1,128]{2,1,0:T(1,128)S(1)}, f32[20,1,128]{2,1,0:T(1,128)S(1)}, u32[]{:S(2)}, u32[]{:S(2)}) collective-permute-start(f32[20,1,128]{2,1,0:T(1,128)S(1)} %get-tuple-element.6), channel_id=1, source_target_pairs={{0,32},{1,33},{2,34},{3,35},{4,36},{5,37},{6,38},{7,39},{8,40},{9,... | collective-permute-start | bytes 30728 | tf_op jit(solution)/shard_map/ppermute | solution.py:196
  71.9 1.9 %collective-permute-start.1 = (f32[20,1,128]{2,1,0:T(1,128)S(1)}, f32[20,1,128]{2,1,0:T(1,128)S(1)}, u32[]{:S(2)}, u32[]{:S(2)}) collective-permute-start(f32[20,1,128]{2,1,0:T(1,128)S(1)} %get-tuple-element.5), channel_id=1, source_target_pairs={{0,64},{1,65},{2,66},{3,67},{4,68},{5,69},{6,70},{7,71},{8,72},{9,... | collective-permute-start | bytes 30728 | tf_op jit(solution)/shard_map/ppermute | solution.py:197
  73.8 0.0 collective-permute-done.first_ref
  73.8 0.0 copy-start.5
  73.8 2.5 %collective-permute-done.1.second_ref = f32[20,1,128]{2,1,0:T(1,128)S(1)} collective-permute-done((f32[20,1,128]{2,1,0:T(1,128)S(1)}, f32[20,1,128]{2,1,0:T(1,128)S(1)}, u32[]{:S(2)}, u32[]{:S(2)}) %collective-permute-start.1) | collective-permute-done | bytes 10272 | tf_op jit(solution)/shard_map/ppermute | solution.py:197
  76.3 0.0 copy-start.6
  76.3 0.0 copy-done.4
  76.3 0.0 copy-done.5
  76.3 0.6 copy-done.6
  76.9 2.8 %stencil.1 = f32[18,64,128]{2,1,0:T(8,128)} custom-call(f32[1280,128]{1,0:T(8,128)} %bitcast.14, f32[20,1,128]{2,1,0:T(1,128)} %copy-done.5, f32[20,1,128]{2,1,0:T(1,128)} %copy-done.6, f32[18,64]{1,0:T(8,128)} %bitcast.17, f32[18,64]{1,0:T(8,128)} %bitcast.18, f32[18,64]{1,0:T(8,128)} %bitcast.19), custom_call_target="tpu_custom_call" | custom-call | tf_op jit(solution)/shard_map/stencil/pallas_call | solution.py:198
  (1 shorter events, 0.0 us)
Async XLA Ops:
  0.0 35.6 %copy-start = (bf16[2304,288]{1,0:T(8,128)(2,1)S(1)}, bf16[2304,288]{1,0:T(8,128)(2,1)}, u32[]{:S(2)}) copy-start(bf16[2304,288]{1,0:T(8,128)(2,1)} %constant.24.clone.back_ref) | copy-start | bytes 3981316
  0.0 35.6 %copy-start.2 = (s32[768]{0:T(1024)S(1)}, s32[768]{0:T(1024)}, u32[]{:S(2)}) copy-start(s32[768]{0:T(1024)} %cut_ref.1) | copy-start | bytes 9220
  0.0 35.6 %copy-start.3 = (s32[768]{0:T(1024)S(1)}, s32[768]{0:T(1024)}, u32[]{:S(2)}) copy-start(s32[768]{0:T(1024)} %cap_ref.1) | copy-start | bytes 9220
  35.6 1.4 %copy-start.1 = (bf16[1152,576]{1,0:T(8,128)(2,1)S(1)}, bf16[1152,576]{1,0:T(8,128)(2,1)}, u32[]{:S(2)}) copy-start(bf16[1152,576]{1,0:T(8,128)(2,1)} %constant.23.clone.forth_ref) | copy-start | bytes 3981316
  40.6 26.5 %all-to-all-start.1 = ((f32[64,20,1,128]{3,2,1,0:T(1,128)}), f32[64,20,1,128]{3,2,1,0:T(1,128)S(1)}, u32[]{:S(2)}, u32[]{:S(2)}) async-start(f32[64,20,1,128]{3,2,1,0:T(1,128)} %bitcast.3), calls=%async_computation.1 | async-start | bytes 1310720 | tf_op jit(solution)/shard_map/all_to_all | solution.py:185
  67.1 9.2 %copy-start.4 = (f32[64,20,1,128]{3,2,1,0:T(1,128)}, f32[64,20,1,128]{3,2,1,0:T(1,128)S(1)}, u32[]{:S(2)}) copy-start(f32[64,20,1,128]{3,2,1,0:T(1,128)S(1)} %all-to-all-done.1) | copy-start | bytes 1966084
  67.1 6.7 %collective-permute-start = (f32[20,1,128]{2,1,0:T(1,128)S(1)}, f32[20,1,128]{2,1,0:T(1,128)S(1)}, u32[]{:S(2)}, u32[]{:S(2)}) collective-permute-start(f32[20,1,128]{2,1,0:T(1,128)S(1)} %get-tuple-element.6), channel_id=1, source_target_pairs={{0,32},{1,33},{2,34},{3,35},{4,36},{5,37},{6,38},{7,39},{8,40},{9,... | collective-permute-start | bytes 30728 | tf_op jit(solution)/shard_map/ppermute | solution.py:196
  71.9 4.4 %collective-permute-start.1 = (f32[20,1,128]{2,1,0:T(1,128)S(1)}, f32[20,1,128]{2,1,0:T(1,128)S(1)}, u32[]{:S(2)}, u32[]{:S(2)}) collective-permute-start(f32[20,1,128]{2,1,0:T(1,128)S(1)} %get-tuple-element.5), channel_id=1, source_target_pairs={{0,64},{1,65},{2,66},{3,67},{4,68},{5,69},{6,70},{7,71},{8,72},{9,... | collective-permute-start | bytes 30728 | tf_op jit(solution)/shard_map/ppermute | solution.py:197
  73.8 2.5 %copy-start.5 = (f32[20,1,128]{2,1,0:T(1,128)}, f32[20,1,128]{2,1,0:T(1,128)S(1)}, u32[]{:S(2)}) copy-start(f32[20,1,128]{2,1,0:T(1,128)S(1)} %collective-permute-done.first_ref) | copy-start | bytes 30724
  76.3 0.6 copy-start.6

commit v2 on v1

--- a/solution.py
+++ b/solution.py
@@ -11,15 +11,17 @@
 
 LEV = 16
 WAVES = 288
-
-
-def split_table(table):
+MIB = 1024 * 1024
+
+
+def pair_table(table, width):
     high = table.astype(ml_dtypes.bfloat16)
     low = (table - high.astype(np.float64)).astype(ml_dtypes.bfloat16)
-    return np.concatenate([high, low], axis=0)
-
-
-def tables(full, cols):
+    blank = np.zeros((table.shape[0], width - 2 * table.shape[1]), ml_dtypes.bfloat16)
+    return np.concatenate([high, low, blank], axis=1)
+
+
+def tables(full, cols, width):
     half = full // 2
     sectors = half // cols
     place = (np.arange(cols)[:, None] + cols * np.arange(sectors)[None, :]).reshape(-1)
@@ -28,9 +30,9 @@
         wave = np.arange(parity, WAVES, 2)
         angle = (wave[:, None] * place[None, :] % full) * (2.0 * np.pi / full)
         made.append(np.concatenate([np.cos(angle), np.sin(angle)], axis=0))
-    forth = np.concatenate([split_table(m) for m in made], axis=0)
-    back = np.concatenate([split_table(m.T) for m in made], axis=0)
-    return forth, back
+    forth = [pair_table(m, 2 * width) for m in made]
+    back = np.concatenate([pair_table(m.T, width) for m in made], axis=1)
+    return np.concatenate(forth + [back], axis=0)
 
 
 def pack_kernel(x_ref, out_ref, held, sems):
@@ -55,20 +57,21 @@
 
 
 def product(table, data):
-    both = jnp.dot(table, data, preferred_element_type=jnp.float32)
-    rows = both.shape[0] // 2
+    both = jnp.dot(table, jnp.concatenate([data, data], axis=0), preferred_element_type=jnp.float32)
     depth = both.shape[1] // 2
-    return (both[:rows, :depth] + both[:rows, depth:]) + (both[rows:, :depth] + both[rows:, depth:])
-
-
-def filter_kernel(cols, peers, cut_ref, cap_ref, x_ref, forth_ref, back_ref, out_ref, even, odd):
+    return both[:, :depth] + both[:, depth:]
+
+
+def filter_kernel(cols, peers, cut_ref, cap_ref, x_ref, table_ref, out_ref, even, odd):
     depth = x_ref.shape[1]
     full = cols * peers
     half = peers // 2
     wide = cols + 2
+    width = table_ref.shape[1] // 2
     row = lax.axis_index("lat") * peers + lax.axis_index("lon")
-    cut = cut_ref[row]
-    cap = cap_ref[row]
+    place = lax.broadcasted_iota(jnp.int32, (1, cut_ref.shape[0]), 1)
+    mine = jnp.where((place == row) & (cap_ref[...].reshape(place.shape) == 1), cut_ref[...].reshape(place.shape), 0)
+    cut = jnp.max(mine.astype(jnp.float32)).astype(jnp.int32)
 
     def emit(j, values):
         out_ref[pl.ds(1 + j, peers, stride=wide), :] = values
@@ -77,12 +80,12 @@
         if j == 0:
             out_ref[pl.ds(wide - 1, peers, stride=wide), :] = pltpu.roll(values, peers - 1, 0)
 
-    @pl.when(cap != 1)
+    @pl.when(cut == 0)
     def _():
         for j in range(cols):
             emit(j, x_ref[pl.ds(j, peers, stride=cols), :])
 
-    @pl.when(cap == 1)
+    @pl.when(cut != 0)
     def _():
         for j in range(cols):
             values = x_ref[pl.ds(j, peers, stride=cols), :]
@@ -92,13 +95,13 @@
                 ref[pl.ds(j * half, half), depth : 2 * depth] = low
         back = []
         for parity, ref in ((0, even), (1, odd)):
-            spectrum = product(forth_ref[pl.ds(parity * 2 * WAVES, 2 * WAVES), :], ref[...])
+            spectrum = product(table_ref[pl.ds(parity * WAVES, WAVES), 0 : 2 * ref.shape[0]], ref[...])
             index = lax.broadcasted_iota(jnp.int32, spectrum.shape, 0)
             count = WAVES // 2
             wave = 2 * jnp.where(index < count, index, index - count) + parity
             weight = jnp.where(wave == 0, 1.0 / full, 2.0 / full)
             spectrum = jnp.where(wave < cut, spectrum * weight, 0.0)
-            table = back_ref[pl.ds(parity * full, full), :]
+            table = table_ref[2 * WAVES :, pl.ds(parity * width, 2 * WAVES)]
             back.append(product(table, jnp.concatenate(halves(spectrum), axis=1)))
         for j in range(cols):
             near = back[0][j * half : (j + 1) * half]
@@ -113,6 +116,8 @@
     size = cols // parts
     lat = lax.axis_index("lat")
     odd = lat % 2 == 1
+    first_edge = jnp.where((lat == 0) | (odd & (lat != n_lat - 1)), 0, 1)
+    second_edge = jnp.where(odd, 1, 0)
     lane = lax.broadcasted_iota(jnp.int32, (rows, depth), 1)
     line = lax.broadcasted_iota(jnp.int32, (rows, depth), 0)
     top = lane % LEV == LEV - 1
@@ -126,7 +131,7 @@
     for j in range(cols):
         line_of.append(g_ref[pl.ds(j + 2, rows, stride=wide), :])
         west, here, east = line_of[j : j + 3]
-        first, second = first_ref[j + 1], second_ref[j + 1]
+        first, second = first_ref[first_edge, j + 1], second_ref[second_edge, j + 1]
         north = north_sign * jnp.where(odd, second, first)
         south = south_sign * jnp.where(odd, first, second)
         up = jnp.where(line == 0, north, pltpu.roll(here, 1, 0))
@@ -153,38 +158,37 @@
     peers = lax.axis_size("lon")
     n_lat = lax.axis_size("lat")
     vmem = pl.BlockSpec(memory_space=pltpu.VMEM)
-    smem = pl.BlockSpec(memory_space=pltpu.SMEM)
     wide = cols + 2
 
     packed = pl.pallas_call(
         pack_kernel,
-        out_shape=jax.ShapeDtypeStruct((rows * cols, depth), jnp.float32),
-        in_specs=[pl.BlockSpec(memory_space=pl.ANY)],
+        out_shape=pltpu.VMEM((rows * cols, depth), jnp.float32),
+        in_specs=[pl.BlockSpec(memory_space=pltpu.HBM)],
         out_specs=vmem,
         scratch_shapes=[pltpu.VMEM((cols, rows, depth), jnp.float32), pltpu.SemaphoreType.DMA((6,))],
+        compiler_params=pltpu.CompilerParams(vmem_limit_bytes=4 * MIB),
+        cost_estimate=pl.CostEstimate(flops=10000000000, bytes_accessed=67108864, transcendentals=0),
         name="pack",
-    )(jnp.transpose(fields, (1, 0, 2)))
+    )(pltpu.with_memory_space_constraint(jnp.transpose(fields, (1, 0, 2)), pltpu.HBM))
     block = lax.all_to_all(packed.reshape(peers, cols, 1, depth), "lon", 0, 0, tiled=True)
-    forth, back = tables(cols * peers, cols)
+    table = tables(cols * peers, cols, 640)
     half = cols * peers // 2
     filtered = pl.pallas_call(
         functools.partial(filter_kernel, cols, peers),
         out_shape=jax.ShapeDtypeStruct((peers * wide, depth), jnp.float32),
-        in_specs=[smem, smem] + [vmem] * 3,
+        in_specs=[vmem] * 4,
         out_specs=vmem,
         scratch_shapes=[pltpu.VMEM((half, 2 * depth), jnp.bfloat16)] * 2,
-        compiler_params=pltpu.CompilerParams(vmem_limit_bytes=24 * 1024 * 1024),
+        compiler_params=pltpu.CompilerParams(vmem_limit_bytes=16 * MIB),
         name="filter",
     )(
         cutoff,
         cap_mask,
         block.reshape(peers * cols, depth),
-        jnp.asarray(forth),
-        jnp.asarray(back),
+        jnp.asarray(table),
     )
     returned = lax.all_to_all(filtered.reshape(peers, wide, 1, depth), "lon", 0, 0, tiled=True)
-    odd = lax.axis_index("lat") % 2 == 1
-    head, tail = returned[0], returned[-1]
+    edges = jnp.stack([returned[0], returned[-1]])
     first, second = [], []
     for lat in range(n_lat):
         for lon in range(peers):
@@ -193,14 +197,15 @@
             inside = 0 <= pair < n_lat
             first.append((here, pair * peers + lon if inside else lat * peers + (lon + peers // 2) % peers))
             second.append((here, (lat ^ 1) * peers + lon))
-    first = lax.ppermute(jnp.where(odd, tail, head), ("lat", "lon"), first)
-    second = lax.ppermute(jnp.where(odd, head, tail), ("lat", "lon"), second)
+    first = lax.ppermute(edges, ("lat", "lon"), first)
+    second = lax.ppermute(edges, ("lat", "lon"), second)
     out = pl.pallas_call(
         functools.partial(stencil_kernel, cols, rows, n_lat),
         out_shape=jax.ShapeDtypeStruct((cols, rows, depth), jnp.float32),
         in_specs=[vmem] * 6,
         out_specs=pl.BlockSpec(memory_space=pl.ANY),
         scratch_shapes=[pltpu.VMEM((cols, rows, depth), jnp.float32), pltpu.SemaphoreType.DMA((6,))],
+        compiler_params=pltpu.CompilerParams(vmem_limit_bytes=8 * MIB),
         name="stencil",
     )(
         returned.reshape(rows * wide, depth),

time: 80.1 us -> 72 us (0.90)
  blocking collectives: 33.4 us -> 58.8 us
  waiting for transfers between devices: 22.6 us -> 1.27 us
  starting transfers between devices: 13 us -> 6.67 us
  Pallas kernels: 8.57 us -> 4.9 us
  local copies, waits for them, and re-layouts: 1.98 us -> 0.02 us
    all_to_all x0 -> x1, blocking collectives: none -> 26.3 us  [per_device(): lax.all_to_all(filtered.reshape(peers, wide, 1, depth), 'lon', 0, 0, tile...]
    all_to_all x1 -> x0, waiting for transfers between devices: 20.1 us -> none  [per_device(): lax.all_to_all(filtered.reshape(peers, wide, 1, depth), 'lon', 0, 0, tile...]
    all_to_all x1 -> x0, starting transfers between devices: 6.34 us -> none  [per_device(): lax.all_to_all(filtered.reshape(peers, wide, 1, depth), 'lon', 0, 0, tile...]
    unnamed x14 -> x12, local copies, waits for them, and re-layouts: 1.98 us -> 0.02 us
    pallas_call x1, Pallas kernels: 3.65 us -> 1.89 us  [per_device(): pl.pallas_call(functools.partial(filter_kernel, cols, peers), out_shape=j...]
    ppermute x2, waiting for transfers between devices: 2.47 us -> 1.27 us  [the longest x1 1.26 us: per_device(): first = lax.ppermute(edges, ('lat', 'lon'), first)]
    pallas_call x1, Pallas kernels: 2.78 us -> 1.68 us  [per_device(): pl.pallas_call(functools.partial(stencil_kernel, cols, rows, n_lat), out_...]
    all_to_all x1, blocking collectives: 33.4 us -> 32.5 us  [per_device(): lax.all_to_all(packed.reshape(peers, cols, 1, depth), 'lon', 0, 0, tiled=...]
  transfers between devices with their start and end apart: 3 -> 2, of which waited for: 2 -> 1; matrix products, arithmetic and copies ran while one was open for 0% -> 0% of each run, Pallas kernels for 0% -> 0%
where the time goes in v2:
time: 72 us; the launch traced here: 71.7 us
  blocking collectives  58.8 us (82%)
  starting transfers between devices  6.67 us (9%)
  Pallas kernels  4.9 us (7%)
  waiting for transfers between devices  1.27 us (2%)
    all_to_all x1, blocking collectives, per_device(): lax.all_to_all(packed.reshape(peers, cols, 1, depth), 'lon', 0, 0, tiled=...  32.5 us
    all_to_all x1, blocking collectives, per_device(): lax.all_to_all(filtered.reshape(peers, wide, 1, depth), 'lon', 0, 0, tile...  26.3 us
    ppermute x1, starting transfers between devices, per_device(): first = lax.ppermute(edges, ('lat', 'lon'), first)  4.75 us
    ppermute x1, starting transfers between devices, per_device(): second = lax.ppermute(edges, ('lat', 'lon'), second)  1.92 us
    pallas_call x1, Pallas kernels, per_device(): pl.pallas_call(functools.partial(filter_kernel, cols, peers), out_shape=j...  1.89 us
    pallas_call x1, Pallas kernels, per_device(): pl.pallas_call(functools.partial(stencil_kernel, cols, rows, n_lat), out_...  1.68 us
  transfers between devices with their start and end apart: 2, of which 1 were waited for; matrix products, arithmetic and copies ran while one was open for 0% of the time, Pallas kernels for 0%

profile of v2, /device:TPU:1, one launch (start us, length us, event | category | flops | bytes accessed | tf_op | source)
XLA Modules:
  0.0 71.7 jit_solution(8798789800217799556)
XLA Ops:
  0.0 0.0 copy-start
  0.0 0.0 copy-start.4
  0.0 0.0 copy-start.5
  0.0 1.3 %pack.1 = f32[1152,128]{1,0:T(8,128)S(1)} custom-call(f32[18,64,128]{2,1,0:T(8,128)} %bitcast.16), custom_call_target="tpu_custom_call" | custom-call | flops 10000000000 | bytes 67108864 | tf_op jit(solution)/shard_map/pack/pallas_call | solution.py:163
  1.4 32.5 %all_to_all.10 = f32[64,18,1,128]{3,2,1,0:T(1,128)S(1)} all-to-all(f32[64,18,1,128]{3,2,1,0:T(1,128)S(1)} %bitcast.12), channel_id=1, replica_groups=mesh['lat'=12,'lon'=64] {'lon'}, dimensions={0} | all-to-all | bytes 1179648 | tf_op jit(solution)/shard_map/all_to_all | solution.py:173
  33.9 0.0 copy-start.1
  33.9 0.0 copy-start.2
  33.9 0.0 copy-start.3
  33.9 0.0 copy-done
  33.9 0.0 copy-done.4
  33.9 0.0 copy-done.5
  33.9 1.9 %filter.1 = f32[1280,128]{1,0:T(8,128)S(1)} custom-call(s32[768]{0:T(1024)S(1)} %copy-done.4, s32[768]{0:T(1024)S(1)} %copy-done.5, f32[1152,128]{1,0:T(8,128)S(1)} %bitcast.11, bf16[1152,1280]{1,0:T(8,128)(2,1)S(1)} %copy-done), custom_call_target="tpu_custom_call" | custom-call | tf_op jit(solution)/shard_map/filter/pallas_call | solution.py:176
  35.8 26.3 %all_to_all.11 = f32[64,20,1,128]{3,2,1,0:T(1,128)S(1)} all-to-all(f32[64,20,1,128]{3,2,1,0:T(1,128)S(1)} %bitcast.10), channel_id=1, replica_groups=mesh['lat'=12,'lon'=64] {'lon'}, dimensions={0} | all-to-all | bytes 1310720 | tf_op jit(solution)/shard_map/all_to_all | solution.py:190
  62.1 1.9 %collective-permute-start.1 = (f32[2,20,1,128]{3,2,1,0:T(1,128)S(1)}, f32[2,20,1,128]{3,2,1,0:T(1,128)S(1)}, u32[]{:S(2)}, u32[]{:S(2)}) collective-permute-start(f32[2,20,1,128]{3,2,1,0:T(1,128)S(1)} %pad_maximum_fusion), channel_id=1, source_target_pairs={{0,64},{1,65},{2,66},{3,67},{4,68},{5,69},{6,70},{7,71},{8,72},{9,... | collective-permute-start | bytes 61448 | tf_op jit(solution)/shard_map/ppermute | solution.py:201
  64.0 4.7 %collective-permute-start = (f32[2,20,1,128]{3,2,1,0:T(1,128)S(1)}, f32[2,20,1,128]{3,2,1,0:T(1,128)S(1)}, u32[]{:S(2)}, u32[]{:S(2)}) collective-permute-start(f32[2,20,1,128]{3,2,1,0:T(1,128)S(1)} %pad_maximum_fusion), channel_id=1, source_target_pairs={{0,32},{1,33},{2,34},{3,35},{4,36},{5,37},{6,38},{7,39},{8,40},{9,... | collective-permute-start | bytes 61448 | tf_op jit(solution)/shard_map/ppermute | solution.py:200
  68.8 0.0 collective-permute-done.1.second_ref
  68.8 1.3 %collective-permute-done.first_ref = f32[2,20,1,128]{3,2,1,0:T(1,128)S(1)} collective-permute-done((f32[2,20,1,128]{3,2,1,0:T(1,128)S(1)}, f32[2,20,1,128]{3,2,1,0:T(1,128)S(1)}, u32[]{:S(2)}, u32[]{:S(2)}) %collective-permute-start) | collective-permute-done | bytes 20512 | tf_op jit(solution)/shard_map/ppermute | solution.py:200
  70.1 0.0 copy-done.1
  70.1 0.0 copy-done.2
  70.1 0.0 copy-done.3
  70.1 1.7 %stencil.1 = f32[18,64,128]{2,1,0:T(8,128)} custom-call(f32[1280,128]{1,0:T(8,128)S(1)} %bitcast.9, f32[2,20,1,128]{3,2,1,0:T(1,128)S(1)} %collective-permute-done.first_ref, f32[2,20,1,128]{3,2,1,0:T(1,128)S(1)} %collective-permute-done.1.second_ref, f32[18,64]{1,0:T(8,128)S(1)} %bitcast.13, f32[18,64]{1,0:T(8,128)S(1)} %bitcast.14, f32[18,64]{1,0:T(8,128)S(1)} %bitcast.15), custom_call_target="tpu_custom_call" | custom-call | tf_op jit(solution)/shard_map/stencil/pallas_call | solution.py:202
  (2 shorter events, 0.0 us)
Async XLA Ops:
  0.0 33.9 %copy-start = (bf16[1152,1280]{1,0:T(8,128)(2,1)S(1)}, bf16[1152,1280]{1,0:T(8,128)(2,1)}, u32[]{:S(2)}) copy-start(bf16[1152,1280]{1,0:T(8,128)(2,1)} %constant.2.clone.table_ref) | copy-start | bytes 8847364
  0.0 33.9 %copy-start.4 = (s32[768]{0:T(1024)S(1)}, s32[768]{0:T(1024)}, u32[]{:S(2)}) copy-start(s32[768]{0:T(1024)} %cut_ref.1) | copy-start | bytes 9220
  0.0 33.9 %copy-start.5 = (s32[768]{0:T(1024)S(1)}, s32[768]{0:T(1024)}, u32[]{:S(2)}) copy-start(s32[768]{0:T(1024)} %cap_ref.1) | copy-start | bytes 9220
  33.9 36.2 %copy-start.1 = (f32[64,18]{0,1:T(8,128)S(1)}, f32[64,18]{0,1:T(8,128)}, u32[]{:S(2)}) copy-start(f32[64,18]{0,1:T(8,128)} %param.10) | copy-start | bytes 13828
  33.9 36.2 %copy-start.2 = (f32[64,18]{0,1:T(8,128)S(1)}, f32[64,18]{0,1:T(8,128)}, u32[]{:S(2)}) copy-start(f32[64,18]{0,1:T(8,128)} %param.11) | copy-start | bytes 13828
  33.9 36.2 %copy-start.3 = (f32[64,18]{0,1:T(8,128)S(1)}, f32[64,18]{0,1:T(8,128)}, u32[]{:S(2)}) copy-start(f32[64,18]{0,1:T(8,128)} %param.12) | copy-start | bytes 13828
  62.1 6.7 %collective-permute-start.1 = (f32[2,20,1,128]{3,2,1,0:T(1,128)S(1)}, f32[2,20,1,128]{3,2,1,0:T(1,128)S(1)}, u32[]{:S(2)}, u32[]{:S(2)}) collective-permute-start(f32[2,20,1,128]{3,2,1,0:T(1,128)S(1)} %pad_maximum_fusion), channel_id=1, source_target_pairs={{0,64},{1,65},{2,66},{3,67},{4,68},{5,69},{6,70},{7,71},{8,72},{9,... | collective-permute-start | bytes 61448 | tf_op jit(solution)/shard_map/ppermute | solution.py:201
  64.0 6.0 %collective-permute-start = (f32[2,20,1,128]{3,2,1,0:T(1,128)S(1)}, f32[2,20,1,128]{3,2,1,0:T(1,128)S(1)}, u32[]{:S(2)}, u32[]{:S(2)}) collective-permute-start(f32[2,20,1,128]{3,2,1,0:T(1,128)S(1)} %pad_maximum_fusion), channel_id=1, source_target_pairs={{0,32},{1,33},{2,34},{3,35},{4,36},{5,37},{6,38},{7,39},{8,40},{9,... | collective-permute-start | bytes 61448 | tf_op jit(solution)/shard_map/ppermute | solution.py:200

commit v3 on v2

--- a/solution.py
+++ b/solution.py
@@ -11,7 +11,9 @@
 
 LEV = 16
 WAVES = 288
+STEPS = 3
 MIB = 1024 * 1024
+TILE = 8
 
 
 def pair_table(table, width):
@@ -35,7 +37,10 @@
     return np.concatenate(forth + [back], axis=0)
 
 
-def pack_kernel(x_ref, out_ref, held, sems):
+def pack_kernel(x_ref, out_ref, odd_ref, even_ref, held, sems):
+    odd = lax.axis_index("lat") % 2 == 1
+    odd_ref[...] = jnp.full(odd_ref.shape, jnp.where(odd, 1.0, 0.0), jnp.float32)
+    even_ref[...] = jnp.full(even_ref.shape, jnp.where(odd, 0.0, 1.0), jnp.float32)
     cols, rows, _ = x_ref.shape
     parts = sems.shape[0]
     size = cols // parts
@@ -93,7 +98,7 @@
                 high, low = halves(folded)
                 ref[pl.ds(j * half, half), 0:depth] = high
                 ref[pl.ds(j * half, half), depth : 2 * depth] = low
-        back = []
+        spectra = []
         for parity, ref in ((0, even), (1, odd)):
             spectrum = product(table_ref[pl.ds(parity * WAVES, WAVES), 0 : 2 * ref.shape[0]], ref[...])
             index = lax.broadcasted_iota(jnp.int32, spectrum.shape, 0)
@@ -101,23 +106,26 @@
             wave = 2 * jnp.where(index < count, index, index - count) + parity
             weight = jnp.where(wave == 0, 1.0 / full, 2.0 / full)
             spectrum = jnp.where(wave < cut, spectrum * weight, 0.0)
-            table = table_ref[2 * WAVES :, pl.ds(parity * width, 2 * WAVES)]
-            back.append(product(table, jnp.concatenate(halves(spectrum), axis=1)))
-        for j in range(cols):
-            near = back[0][j * half : (j + 1) * half]
-            far = back[1][j * half : (j + 1) * half]
-            emit(j, jnp.concatenate([near + far, near - far], axis=0))
-
-
-def stencil_kernel(cols, rows, n_lat, g_ref, first_ref, second_ref, cl_ref, ct_ref, cv_ref, out_ref, made, sems):
+            spectra.append(jnp.concatenate(halves(spectrum), axis=1))
+        step = cols // STEPS
+        for i in range(STEPS):
+            part = pl.ds(2 * WAVES + i * step * half, step * half)
+            back = [
+                product(table_ref[part, parity * width : parity * width + 2 * WAVES], spectra[parity]) for parity in (0, 1)
+            ]
+            for j in range(step):
+                near = back[0][j * half : (j + 1) * half]
+                far = back[1][j * half : (j + 1) * half]
+                emit(i * step + j, jnp.concatenate([near + far, near - far], axis=0))
+
+
+def stencil_kernel(cols, rows, n_lat, g_ref, cl_ref, ct_ref, cv_ref, out_ref, rim_ref, share_ref, made, sems):
     wide = cols + 2
     depth = g_ref.shape[1]
     parts = sems.shape[0]
     size = cols // parts
     lat = lax.axis_index("lat")
-    odd = lat % 2 == 1
-    first_edge = jnp.where((lat == 0) | (odd & (lat != n_lat - 1)), 0, 1)
-    second_edge = jnp.where(odd, 1, 0)
+    inner = pl.ds(TILE, rows - 2 * TILE)
     lane = lax.broadcasted_iota(jnp.int32, (rows, depth), 1)
     line = lax.broadcasted_iota(jnp.int32, (rows, depth), 0)
     top = lane % LEV == LEV - 1
@@ -131,24 +139,47 @@
     for j in range(cols):
         line_of.append(g_ref[pl.ds(j + 2, rows, stride=wide), :])
         west, here, east = line_of[j : j + 3]
-        first, second = first_ref[first_edge, j + 1], second_ref[second_edge, j + 1]
-        north = north_sign * jnp.where(odd, second, first)
-        south = south_sign * jnp.where(odd, first, second)
-        up = jnp.where(line == 0, north, pltpu.roll(here, 1, 0))
-        down = jnp.where(line == rows - 1, south, pltpu.roll(here, rows - 1, 0))
+        up = jnp.where(line == 0, 0.0, pltpu.roll(here, 1, 0))
+        down = jnp.where(line == rows - 1, 0.0, pltpu.roll(here, rows - 1, 0))
         above = jnp.where(top, 0.0, pltpu.roll(here, depth - 1, 1))
         below = jnp.where(bottom, 0.0, pltpu.roll(here, 1, 1))
         twice = 2.0 * here
-        made[j] = (
+        lat_share = coefs[1][:, j : j + 1]
+        value = (
             here
             + coefs[0][:, j : j + 1] * (east + west - twice)
-            + coefs[1][:, j : j + 1] * (up + down - twice)
+            + lat_share * (up + down - twice)
             + coefs[2][:, j : j + 1] * (above + below - twice)
         )
+        made[j] = value
+        rim_ref[0, j] = value[:TILE]
+        rim_ref[1, j] = value[rows - TILE :]
+        share_ref[0, j] = lat_share[:1] * north_sign
+        share_ref[1, j] = lat_share[rows - 1 :] * south_sign
         if (j + 1) % size == 0:
             part = pl.ds(j + 1 - size, size)
-            copies.append(pltpu.make_async_copy(made.at[part], out_ref.at[part], sems.at[j // size]))
+            copies.append(pltpu.make_async_copy(made.at[part, inner], out_ref.at[part, inner], sems.at[j // size]))
             copies[-1].start()
+    for copy in copies:
+        copy.wait()
+
+
+def rim_kernel(cols, _, rim_ref, share_ref, first_ref, second_ref, out_ref, made, sems):
+    rows = out_ref.shape[1]
+    odd = lax.axis_index("lat") % 2 == 1
+    line = lax.broadcasted_iota(jnp.int32, rim_ref.shape[2:], 0)
+    for j in range(cols):
+        first, second = first_ref[j], second_ref[j]
+        north = share_ref[0, j] * jnp.where(odd, second, first)
+        south = share_ref[1, j] * jnp.where(odd, first, second)
+        made[0, j] = rim_ref[0, j] + jnp.where(line == 0, north, 0.0)
+        made[1, j] = rim_ref[1, j] + jnp.where(line == TILE - 1, south, 0.0)
+    copies = [
+        pltpu.make_async_copy(made.at[edge], out_ref.at[:, pl.ds(edge * (rows - TILE), TILE)], sems.at[edge])
+        for edge in (0, 1)
+    ]
+    for copy in copies:
+        copy.start()
     for copy in copies:
         copy.wait()
 
@@ -158,13 +189,18 @@
     peers = lax.axis_size("lon")
     n_lat = lax.axis_size("lat")
     vmem = pl.BlockSpec(memory_space=pltpu.VMEM)
+    hbm = pl.BlockSpec(memory_space=pltpu.HBM)
     wide = cols + 2
 
-    packed = pl.pallas_call(
+    packed, odd, even = pl.pallas_call(
         pack_kernel,
-        out_shape=pltpu.VMEM((rows * cols, depth), jnp.float32),
+        out_shape=(
+            pltpu.VMEM((rows * cols, depth), jnp.float32),
+            pltpu.VMEM((1, 1, depth), jnp.float32),
+            pltpu.VMEM((1, 1, depth), jnp.float32),
+        ),
         in_specs=[pl.BlockSpec(memory_space=pltpu.HBM)],
-        out_specs=vmem,
+        out_specs=(vmem, vmem, vmem),
         scratch_shapes=[pltpu.VMEM((cols, rows, depth), jnp.float32), pltpu.SemaphoreType.DMA((6,))],
         compiler_params=pltpu.CompilerParams(vmem_limit_bytes=4 * MIB),
         cost_estimate=pl.CostEstimate(flops=10000000000, bytes_accessed=67108864, transcendentals=0),
@@ -188,6 +224,7 @@
         jnp.asarray(table),
     )
     returned = lax.all_to_all(filtered.reshape(peers, wide, 1, depth), "lon", 0, 0, tiled=True)
+    head, tail = returned[0, 1:-1], returned[-1, 1:-1]
     edges = jnp.stack([returned[0], returned[-1]])
     first, second = [], []
     for lat in range(n_lat):
@@ -197,24 +234,33 @@
             inside = 0 <= pair < n_lat
             first.append((here, pair * peers + lon if inside else lat * peers + (lon + peers // 2) % peers))
             second.append((here, (lat ^ 1) * peers + lon))
-    first = lax.ppermute(edges, ("lat", "lon"), first)
-    second = lax.ppermute(edges, ("lat", "lon"), second)
-    out = pl.pallas_call(
+    first = lax.ppermute(odd * tail + even * head, ("lat", "lon"), first)
+    second = lax.ppermute(odd * head + even * tail, ("lat", "lon"), second)
+    rim_shape = (2, cols, TILE, depth)
+    out, rim, share = pl.pallas_call(
         functools.partial(stencil_kernel, cols, rows, n_lat),
-        out_shape=jax.ShapeDtypeStruct((cols, rows, depth), jnp.float32),
-        in_specs=[vmem] * 6,
-        out_specs=pl.BlockSpec(memory_space=pl.ANY),
+        out_shape=(
+            pltpu.HBM((cols, rows, depth), jnp.float32),
+            pltpu.VMEM(rim_shape, jnp.float32),
+            pltpu.VMEM((2, cols, 1, depth), jnp.float32),
+        ),
+        in_specs=[vmem] * 4,
+        out_specs=(hbm, vmem, vmem),
         scratch_shapes=[pltpu.VMEM((cols, rows, depth), jnp.float32), pltpu.SemaphoreType.DMA((6,))],
         compiler_params=pltpu.CompilerParams(vmem_limit_bytes=8 * MIB),
+        cost_estimate=pl.CostEstimate(flops=10**9, bytes_accessed=2 * MIB, transcendentals=0),
         name="stencil",
-    )(
-        returned.reshape(rows * wide, depth),
-        first,
-        second,
-        jnp.transpose(coef_lon),
-        jnp.transpose(coef_lat),
-        jnp.transpose(coef_vert),
-    )
+    )(returned.reshape(rows * wide, depth), jnp.transpose(coef_lon), jnp.transpose(coef_lat), jnp.transpose(coef_vert))
+    out = pl.pallas_call(
+        functools.partial(rim_kernel, cols),
+        out_shape=jax.ShapeDtypeStruct((cols, rows, depth), jnp.float32),
+        in_specs=[hbm] + [vmem] * 4,
+        out_specs=hbm,
+        scratch_shapes=[pltpu.VMEM(rim_shape, jnp.float32), pltpu.SemaphoreType.DMA((2,))],
+        input_output_aliases={0: 0},
+        compiler_params=pltpu.CompilerParams(vmem_limit_bytes=4 * MIB),
+        name="rim",
+    )(out, rim, share, first, second)
     return jnp.transpose(out, (1, 0, 2))
 
 

time: 72 us -> 71 us (0.986)
  waiting for transfers between devices: 1.27 us -> 0.01 us
    ppermute x2, waiting for transfers between devices: 1.27 us -> 0.01 us  [the longest x1 0.01 us: per_device(): second = lax.ppermute(odd * head + even * tail, ('lat', 'lon'), second)]
    pallas_call x1 -> x2, Pallas kernels: 1.34 us -> 2.07 us  [the longest x1 1.34 us: per_device(): pl.pallas_call(pack_kernel, out_shape=(pltpu.VMEM((rows * cols, depth), j...]
  transfers between devices with their start and end apart: 2 -> 2, of which waited for: 1 -> 0; matrix products, arithmetic and copies ran while one was open for 0% -> 0% of each run, Pallas kernels for 0% -> 2%
where the time goes in v3:
time: 71 us; the launch traced here: 70.7 us
  blocking collectives  58.8 us (83%)
  starting transfers between devices  6.67 us (9%)
  Pallas kernels  5.12 us (7%)
    all_to_all x1, blocking collectives, per_device(): lax.all_to_all(packed.reshape(peers, cols, 1, depth), 'lon', 0, 0, tiled=...  32.5 us
    all_to_all x1, blocking collectives, per_device(): lax.all_to_all(filtered.reshape(peers, wide, 1, depth), 'lon', 0, 0, tile...  26.3 us
    ppermute x1, starting transfers between devices, per_device(): first = lax.ppermute(odd * tail + even * head, ('lat', 'lon'), first)  4.75 us
    ppermute x1, starting transfers between devices, per_device(): second = lax.ppermute(odd * head + even * tail, ('lat', 'lon'), second)  1.92 us
    pallas_call x1, Pallas kernels, per_device(): pl.pallas_call(functools.partial(stencil_kernel, cols, rows, n_lat), out_...  1.67 us
  transfers between devices with their start and end apart: 2, of which 0 were waited for; matrix products, arithmetic and copies ran while one was open for 0% of the time, Pallas kernels for 2%

profile of v3, /device:TPU:1, one launch (start us, length us, event | category | flops | bytes accessed | tf_op | source)
XLA Modules:
  0.0 70.7 jit_solution(10939878688084903561)
XLA Ops:
  0.0 0.0 copy-start
  0.0 0.0 copy-start.1
  0.0 0.0 copy-start.2
  0.0 1.3 %pack.1 = (f32[1152,128]{1,0:T(8,128)S(1)}, f32[1,1,128]{2,1,0:T(1,128)S(1)}, f32[1,1,128]{2,1,0:T(1,128)S(1)}) custom-call(f32[18,64,128]{2,1,0:T(8,128)} %bitcast.32), custom_call_target="tpu_custom_call" | custom-call | flops 10000000000 | bytes 67108864 | tf_op jit(solution)/shard_map/pack/pallas_call | solution.py:195
  1.4 32.5 %all_to_all.10 = f32[64,18,1,128]{3,2,1,0:T(1,128)S(1)} all-to-all(f32[64,18,1,128]{3,2,1,0:T(1,128)S(1)} %bitcast.26), channel_id=1, replica_groups=mesh['lat'=12,'lon'=64] {'lon'}, dimensions={0} | all-to-all | bytes 1179648 | tf_op jit(solution)/shard_map/all_to_all | solution.py:209
  33.9 0.0 copy-start.3
  33.9 0.0 copy-start.4
  33.9 0.0 copy-start.5
  33.9 0.0 copy-done
  33.9 0.0 copy-done.1
  33.9 0.0 copy-done.2
  33.9 1.4 %filter.1 = f32[1280,128]{1,0:T(8,128)S(1)} custom-call(s32[768]{0:T(1024)S(1)} %copy-done.1, s32[768]{0:T(1024)S(1)} %copy-done.2, f32[1152,128]{1,0:T(8,128)S(1)} %bitcast.24, bf16[1152,1280]{1,0:T(8,128)(2,1)S(1)} %copy-done), custom_call_target="tpu_custom_call" | custom-call | tf_op jit(solution)/shard_map/filter/pallas_call | solution.py:212
  35.3 26.3 %all_to_all.11 = f32[64,20,1,128]{3,2,1,0:T(1,128)S(1)} all-to-all(f32[64,20,1,128]{3,2,1,0:T(1,128)S(1)} %bitcast.23), channel_id=1, replica_groups=mesh['lat'=12,'lon'=64] {'lon'}, dimensions={0} | all-to-all | bytes 1310720 | tf_op jit(solution)/shard_map/all_to_all | solution.py:226
  61.6 1.9 %collective-permute-start.1 = (f32[18,1,128]{2,1,0:T(1,128)S(1)}, f32[18,1,128]{2,1,0:T(1,128)S(1)}, u32[]{:S(2)}, u32[]{:S(2)}) collective-permute-start(f32[18,1,128]{2,1,0:T(1,128)S(1)} %get-tuple-element.17), channel_id=1, source_target_pairs={{0,64},{1,65},{2,66},{3,67},{4,68},{5,69},{6,70},{7,71},{8,72},{9,... | collective-permute-start | bytes 27656 | tf_op jit(solution)/shard_map/ppermute | solution.py:238
  63.5 4.7 %collective-permute-start = (f32[18,1,128]{2,1,0:T(1,128)S(1)}, f32[18,1,128]{2,1,0:T(1,128)S(1)}, u32[]{:S(2)}, u32[]{:S(2)}) collective-permute-start(f32[18,1,128]{2,1,0:T(1,128)S(1)} %get-tuple-element.18), channel_id=1, source_target_pairs={{0,32},{1,33},{2,34},{3,35},{4,36},{5,37},{6,38},{7,39},{8,40},{9,... | collective-permute-start | bytes 27656 | tf_op jit(solution)/shard_map/ppermute | solution.py:237
  68.3 0.0 copy-done.3
  68.3 0.0 copy-done.4
  68.3 0.0 copy-done.5
  68.3 1.7 %stencil.1 = (f32[18,64,128]{2,1,0:T(8,128)}, f32[2,18,8,128]{3,2,1,0:T(8,128)S(1)}, f32[2,18,1,128]{3,2,1,0:T(1,128)S(1)}) custom-call(f32[1280,128]{1,0:T(8,128)S(1)} %bitcast.25, f32[18,64]{1,0:T(8,128)S(1)} %bitcast.29, f32[18,64]{1,0:T(8,128)S(1)} %bitcast.30, f32[18,64]{1,0:T(8,128)S(1)} %bitcast.31), custom_call_target="tpu_custom_call" | custom-call | flops 1000000000 | bytes 2097152 | tf_op jit(solution)/shard_map/stencil/pallas_call | solution.py:240
  70.0 0.0 collective-permute-done.1.second_ref
  70.0 0.0 collective-permute-done.first_ref
  70.0 0.7 %rim.1 = f32[18,64,128]{2,1,0:T(8,128)} custom-call(f32[18,64,128]{2,1,0:T(8,128)} %get-tuple-element.12._, f32[2,18,8,128]{3,2,1,0:T(8,128)S(1)} %get-tuple-element.13.rim_ref, f32[2,18,1,128]{3,2,1,0:T(1,128)S(1)} %get-tuple-element.14.share_ref, f32[18,1,128]{2,1,0:T(1,128)S(1)} %collective-permute-done.first_ref, ...), custom_call_target="tpu_custom_call", output_to_operand_aliasing={{}: (0, {})} | custom-call | tf_op jit(solution)/shard_map/rim/pallas_call | solution.py:254
  (1 shorter events, 0.0 us)
Async XLA Ops:
  0.0 33.9 %copy-start = (bf16[1152,1280]{1,0:T(8,128)(2,1)S(1)}, bf16[1152,1280]{1,0:T(8,128)(2,1)}, u32[]{:S(2)}) copy-start(bf16[1152,1280]{1,0:T(8,128)(2,1)} %constant.2.clone.table_ref) | copy-start | bytes 8847364
  0.0 33.9 %copy-start.1 = (s32[768]{0:T(1024)S(1)}, s32[768]{0:T(1024)}, u32[]{:S(2)}) copy-start(s32[768]{0:T(1024)} %cut_ref.1) | copy-start | bytes 9220
  0.0 33.9 %copy-start.2 = (s32[768]{0:T(1024)S(1)}, s32[768]{0:T(1024)}, u32[]{:S(2)}) copy-start(s32[768]{0:T(1024)} %cap_ref.1) | copy-start | bytes 9220
  33.9 34.4 %copy-start.3 = (f32[64,18]{0,1:T(8,128)S(1)}, f32[64,18]{0,1:T(8,128)}, u32[]{:S(2)}) copy-start(f32[64,18]{0,1:T(8,128)} %param.10) | copy-start | bytes 13828
  33.9 34.4 %copy-start.4 = (f32[64,18]{0,1:T(8,128)S(1)}, f32[64,18]{0,1:T(8,128)}, u32[]{:S(2)}) copy-start(f32[64,18]{0,1:T(8,128)} %param.11) | copy-start | bytes 13828
  33.9 34.4 %copy-start.5 = (f32[64,18]{0,1:T(8,128)S(1)}, f32[64,18]{0,1:T(8,128)}, u32[]{:S(2)}) copy-start(f32[64,18]{0,1:T(8,128)} %param.12) | copy-start | bytes 13828
  61.6 8.4 %collective-permute-start.1 = (f32[18,1,128]{2,1,0:T(1,128)S(1)}, f32[18,1,128]{2,1,0:T(1,128)S(1)}, u32[]{:S(2)}, u32[]{:S(2)}) collective-permute-start(f32[18,1,128]{2,1,0:T(1,128)S(1)} %get-tuple-element.17), channel_id=1, source_target_pairs={{0,64},{1,65},{2,66},{3,67},{4,68},{5,69},{6,70},{7,71},{8,72},{9,... | collective-permute-start | bytes 27656 | tf_op jit(solution)/shard_map/ppermute | solution.py:238
  63.5 6.5 %collective-permute-start = (f32[18,1,128]{2,1,0:T(1,128)S(1)}, f32[18,1,128]{2,1,0:T(1,128)S(1)}, u32[]{:S(2)}, u32[]{:S(2)}) collective-permute-start(f32[18,1,128]{2,1,0:T(1,128)S(1)} %get-tuple-element.18), channel_id=1, source_target_pairs={{0,32},{1,33},{2,34},{3,35},{4,36},{5,37},{6,38},{7,39},{8,40},{9,... | collective-permute-start | bytes 27656 | tf_op jit(solution)/shard_map/ppermute | solution.py:237

commit v4 on v3

v4 whole, which is shorter than its diff:
```python
import functools

import jax
import jax.numpy as jnp
import ml_dtypes
import numpy as np
from jax import lax
from jax.experimental import pallas as pl
from jax.experimental.pallas import tpu as pltpu
from jax.sharding import PartitionSpec as P

LEV = 16
WAVES = 288
BACK_WIDTH = 384
STEPS = 1
MIB = 1024 * 1024
TILE = 8
LATE = 12


def pair_table(table, width):
    high = table.astype(ml_dtypes.bfloat16)
    low = (table - high.astype(np.float64)).astype(ml_dtypes.bfloat16)
    blank = np.zeros((table.shape[0], width - 2 * table.shape[1]), ml_dtypes.bfloat16)
    return np.concatenate([high, low, blank], axis=1)


def ring(peers):
    count = peers // 4
    return [q * count + (count - 1 - i if q % 2 else i) for q in range(4) for i in range(count)]


def pairs(cols):
    return [j for i in range(cols // 2) for j in (i, cols - 1 - i)]


def tables(full, cols):
    sectors = full // cols // 4
    forth, back = [], []
    for parity in (0, 1):
        for curve in (np.cos, np.sin):
            for made, columns in ((forth, np.arange(cols)), (back, np.array(pairs(cols)))):
                place = (columns[:, None] + cols * np.arange(sectors)[None, :]).reshape(-1)
                wave = np.arange(parity, WAVES, 2)
                made.append(curve(wave[:, None] * (2 * place[None, :] + 1) % (2 * full) * (np.pi / full)))
    width = 2 * BACK_WIDTH
    below = [np.concatenate([pair_table(m.T, BACK_WIDTH) for m in back[i : i + 2]], axis=1) for i in (0, 2)]
    return np.concatenate([pair_table(m, width) for m in forth] + below, axis=0)


def pack_kernel(x_ref, out_ref, odd_ref, even_ref, held, sems):
    odd = lax.axis_index("lat") % 2 == 1
    odd_ref[...] = jnp.full(odd_ref.shape, jnp.where(odd, 1.0, 0.0), jnp.float32)
    even_ref[...] = jnp.full(even_ref.shape, jnp.where(odd, 0.0, 1.0), jnp.float32)
    cols, rows, _ = x_ref.shape
    parts = sems.shape[0]
    size = cols // parts
    copies = []
    for i in range(parts):
        part = pl.ds(i * size, size)
        copies.append(pltpu.make_async_copy(x_ref.at[part], held.at[part], sems.at[i]))
        copies[-1].start()
    for i in range(parts):
        copies[i].wait()
        for j in range(i * size, (i + 1) * size):
            out_ref[pl.ds(j, rows, stride=cols), :] = held[j]


def halves(values):
    high = values.astype(jnp.bfloat16)
    low = (values - high.astype(jnp.float32)).astype(jnp.bfloat16)
    return high, low


def product(table, data):
    both = jnp.dot(table, jnp.concatenate([data, data], axis=0), preferred_element_type=jnp.float32)
    depth = both.shape[1] // 2
    return both[:, :depth] + both[:, depth:]


def filter_kernel(cols, peers, cut_ref, cap_ref, x_ref, table_ref, out_ref, folds):
    depth = x_ref.shape[1]
    full = cols * peers
    count = peers // 4
    wide = cols + 2
    waves = WAVES // 2
    quarter = cols * count
    sector = lax.axis_index("lon")
    turn = sector // count
    place = jnp.where(turn % 2 == 1, (2 * turn + 1) * count - 1 - sector, sector)
    row = lax.axis_index("lat") * peers + place
    line = lax.broadcasted_iota(jnp.int32, (1, cut_ref.shape[0]), 1)
    mine = jnp.where((line == row) & (cap_ref[...].reshape(line.shape) == 1), cut_ref[...].reshape(line.shape), 0)
    cut = jnp.max(mine.astype(jnp.float32)).astype(jnp.int32)
    index = lax.broadcasted_iota(jnp.int32, (count, depth), 0)

    def lower(block, first):
        return jnp.where(index == 0, first, pltpu.roll(block, 1, 0))

    def upper(block, last):
        return jnp.where(index == count - 1, last, pltpu.roll(block, count - 1, 0))

    def emit(j, blocks):
        a, b, c, d = blocks
        rows = [(1 + j, blocks)]
        if j == cols - 1:
            rows.append((0, (lower(a, d[:1]), upper(b, a[-1:]), lower(c, b[:1]), upper(d, c[-1:]))))
        if j == 0:
            rows.append((wide - 1, (upper(a, b[-1:]), lower(b, c[:1]), upper(c, d[-1:]), lower(d, a[:1]))))
        for i, values in rows:
            out_ref[pl.ds(i, peers, stride=wide), :] = jnp.concatenate(values, axis=0)

    def column(j):
        return [x_ref[pl.ds(q * quarter + j, count, stride=cols), :] for q in range(4)]

    @pl.when(cut == 0)
    def _():
        for j in range(cols):
            emit(j, column(j))

    @pl.when(cut != 0)
    def _():
        for j in range(cols):
            a, _, c, _ = column(j)
            _, b, _, d = column(cols - 1 - j)
            for parity, (here, mirror) in enumerate(((a + c, d + b), (a - c, d - b))):
                for kind, folded in enumerate((here + mirror, here - mirror)):
                    high, low = halves(folded)
                    part = pl.ds(j * count, count)
                    folds[2 * parity + kind, part, 0:depth] = high
                    folds[2 * parity + kind, part, depth : 2 * depth] = low
        spectra = []
        for i in range(4):
            spectrum = product(table_ref[pl.ds(i * waves, waves), 0 : 2 * quarter], folds[i])
            wave = 2 * lax.broadcasted_iota(jnp.int32, spectrum.shape, 0) + i // 2
            weight = jnp.where(wave == 0, 1.0 / full, 2.0 / full)
            spectrum = jnp.where(wave < cut, spectrum * weight, 0.0)
            spectra.append(jnp.concatenate(halves(spectrum), axis=1))
        step = cols // STEPS
        order = pairs(cols)
        for k in range(STEPS):
            parts = []
            for i in range(4):
                part = pl.ds(4 * waves + i // 2 * quarter + k * step * count, step * count)
                start = i % 2 * BACK_WIDTH
                parts.append(product(table_ref[part, start : start + 2 * waves], spectra[i]))
            made = {}
            for t in range(step):
                ce, se, co, so = [p[t * count : (t + 1) * count] for p in parts]
                j = order[k * step + t]
                made[j, 0], made[cols - 1 - j, 3] = (ce + co) + (se + so), (ce + co) - (se + so)
                made[j, 2], made[cols - 1 - j, 1] = (ce - co) + (se - so), (ce - co) - (se - so)
                if t % 2 == 1:
                    for i in (order[k * step + t - 1], j):
                        emit(i, [made[i, q] for q in range(4)])


def stencil_kernel(cols, rows, n_lat, g_ref, cl_ref, ct_ref, cv_ref, out_ref, rim_ref, share_ref, late_ref, made, sems):
    wide = cols + 2
    depth = g_ref.shape[1]
    early = made.shape[0]
    size = early // sems.shape[0]
    lat = lax.axis_index("lat")
    inner = pl.ds(TILE, rows - 2 * TILE)
    lane = lax.broadcasted_iota(jnp.int32, (rows, depth), 1)
    line = lax.broadcasted_iota(jnp.int32, (rows, depth), 0)
    top = lane % LEV == LEV - 1
    bottom = lane % LEV == 0
    flip = jnp.where(lax.broadcasted_iota(jnp.int32, (1, depth), 1) < 2 * LEV, -1.0, 1.0)
    north_sign = jnp.where(lat == 0, flip, 1.0)
    south_sign = jnp.where(lat == n_lat - 1, flip, 1.0)
    coefs = [jnp.transpose(ref[...]) for ref in (cl_ref, ct_ref, cv_ref)]
    line_of = [g_ref[pl.ds(i, rows, stride=wide), :] for i in range(2)]
    copies = []
    for j in range(cols):
        line_of.append(g_ref[pl.ds(j + 2, rows, stride=wide), :])
        west, here, east = line_of[j : j + 3]
        up = jnp.where(line == 0, 0.0, pltpu.roll(here, 1, 0))
        down = jnp.where(line == rows - 1, 0.0, pltpu.roll(here, rows - 1, 0))
        above = jnp.where(top, 0.0, pltpu.roll(here, depth - 1, 1))
        below = jnp.where(bottom, 0.0, pltpu.roll(here, 1, 1))
        twice = 2.0 * here
        lat_share = coefs[1][:, j : j + 1]
        value = (
            here
            + coefs[0][:, j : j + 1] * (east + west - twice)
            + lat_share * (up + down - twice)
            + coefs[2][:, j : j + 1] * (above + below - twice)
        )
        if j < early:
            made[j] = value[TILE : rows - TILE]
        else:
            late_ref[j - early] = value[TILE : rows - TILE]
        rim_ref[0, j] = value[:TILE]
        rim_ref[1, j] = value[rows - TILE :]
        share_ref[0, j] = lat_share[:1] * north_sign
        share_ref[1, j] = lat_share[rows - 1 :] * south_sign
        if j < early and (j + 1) % size == 0:
            part = pl.ds(j + 1 - size, size)
            copies.append(pltpu.make_async_copy(made.at[part], out_ref.at[part, inner], sems.at[j // size]))
            copies[-1].start()
    for copy in copies:
        copy.wait()


def rim_kernel(cols, _, rim_ref, share_ref, late_ref, first_ref, second_ref, out_ref, made, sems):
    rows = out_ref.shape[1]
    late = pl.ds(cols - late_ref.shape[0], late_ref.shape[0])
    copies = [pltpu.make_async_copy(late_ref, out_ref.at[late, pl.ds(TILE, rows - 2 * TILE)], sems.at[2])]
    copies[0].start()
    odd = lax.axis_index("lat") % 2 == 1
    line = lax.broadcasted_iota(jnp.int32, rim_ref.shape[2:], 0)
    for j in range(cols):
        first, second = first_ref[j], second_ref[j]
        north = share_ref[0, j] * jnp.where(odd, second, first)
        south = share_ref[1, j] * jnp.where(odd, first, second)
        made[0, j] = rim_ref[0, j] + jnp.where(line == 0, north, 0.0)
        made[1, j] = rim_ref[1, j] + jnp.where(line == TILE - 1, south, 0.0)
    for edge in (0, 1):
        there = out_ref.at[:, pl.ds(edge * (rows - TILE), TILE)]
        copies.append(pltpu.make_async_copy(made.at[edge], there, sems.at[edge]))
        copies[-1].start()
    for copy in copies:
        copy.wait()


def per_device(fields, cutoff, cap_mask, coef_lon, coef_lat, coef_vert):
    rows, cols, depth = fields.shape
    peers = lax.axis_size("lon")
    n_lat = lax.axis_size("lat")
    vmem = pl.BlockSpec(memory_space=pltpu.VMEM)
    hbm = pl.BlockSpec(memory_space=pltpu.HBM)
    wide = cols + 2

    packed, odd, even = pl.pallas_call(
        pack_kernel,
        out_shape=(
            pltpu.VMEM((rows * cols, depth), jnp.float32),
            pltpu.VMEM((1, 1, depth), jnp.float32),
            pltpu.VMEM((1, 1, depth), jnp.float32),
        ),
        in_specs=[pl.BlockSpec(memory_space=pltpu.HBM)],
        out_specs=(vmem, vmem, vmem),
        scratch_shapes=[pltpu.VMEM((cols, rows, depth), jnp.float32), pltpu.SemaphoreType.DMA((2,))],
        compiler_params=pltpu.CompilerParams(vmem_limit_bytes=4 * MIB),
        cost_estimate=pl.CostEstimate(flops=10000000000, bytes_accessed=67108864, transcendentals=0),
        name="pack",
    )(pltpu.with_memory_space_constraint(jnp.transpose(fields, (1, 0, 2)), pltpu.HBM))
    order = [ring(peers)]
    block = lax.all_to_all(packed.reshape(peers, cols, 1, depth), "lon", 0, 0, axis_index_groups=order, tiled=True)
    table = tables(cols * peers, cols)
    filtered = pl.pallas_call(
        functools.partial(filter_kernel, cols, peers),
        out_shape=jax.ShapeDtypeStruct((peers * wide, depth), jnp.float32),
        in_specs=[vmem] * 4,
        out_specs=vmem,
        scratch_shapes=[pltpu.VMEM((4, cols * peers // 4, 2 * depth), jnp.bfloat16)],
        compiler_params=pltpu.CompilerParams(vmem_limit_bytes=16 * MIB),
        name="filter",
    )(
        cutoff,
        cap_mask,
        block.reshape(peers * cols, depth),
        jnp.asarray(table),
    )
    returned = lax.all_to_all(
        filtered.reshape(peers, wide, 1, depth), "lon", 0, 0, axis_index_groups=order, tiled=True
    )
    head, tail = returned[0, 1:-1], returned[-1, 1:-1]
    first, second = [], []
    for lat in range(n_lat):
        for lon in range(peers):
            here = lat * peers + lon
            pair = lat + 1 if lat % 2 else lat - 1
            inside = 0 <= pair < n_lat
            first.append((here, pair * peers + lon if inside else lat * peers + (lon + peers // 2) % peers))
            second.append((here, (lat ^ 1) * peers + lon))
    first = lax.ppermute(odd * tail + even * head, ("lat", "lon"), first)
    second = lax.ppermute(odd * head + even * tail, ("lat", "lon"), second)
    rim_shape = (2, cols, TILE, depth)
    out, rim, share, late = pl.pallas_call(
        functools.partial(stencil_kernel, cols, rows, n_lat),
        out_shape=(
            pltpu.HBM((cols, rows, depth), jnp.float32),
            pltpu.VMEM(rim_shape, jnp.float32),
            pltpu.VMEM((2, cols, 1, depth), jnp.float32),
            pltpu.VMEM((LATE, rows - 2 * TILE, depth), jnp.float32),
        ),
        in_specs=[vmem] * 4,
        out_specs=(hbm, vmem, vmem, vmem),
        scratch_shapes=[
            pltpu.VMEM((cols - LATE, rows - 2 * TILE, depth), jnp.float32),
            pltpu.SemaphoreType.DMA((3,)),
        ],
        compiler_params=pltpu.CompilerParams(vmem_limit_bytes=8 * MIB),
        cost_estimate=pl.CostEstimate(flops=10**9, bytes_accessed=2 * MIB, transcendentals=0),
        name="stencil",
    )(returned.reshape(rows * wide, depth), jnp.transpose(coef_lon), jnp.transpose(coef_lat), jnp.transpose(coef_vert))
    out = pl.pallas_call(
        functools.partial(rim_kernel, cols),
        out_shape=jax.ShapeDtypeStruct((cols, rows, depth), jnp.float32),
        in_specs=[hbm] + [vmem] * 5,
        out_specs=hbm,
        scratch_shapes=[pltpu.VMEM(rim_shape, jnp.float32), pltpu.SemaphoreType.DMA((3,))],
        input_output_aliases={0: 0},
        compiler_params=pltpu.CompilerParams(vmem_limit_bytes=4 * MIB),
        name="rim",
    )(out, rim, share, late, first, second)
    return jnp.transpose(out, (1, 0, 2))


def solution(mesh):
    return jax.shard_map(
        per_device,
        mesh=mesh,
        in_specs=(
            P("lat", "lon", None),
            P(),
            P(),
            P("lat", "lon"),
            P("lat", "lon"),
            P("lat", "lon"),
        ),
        out_specs=P("lat", "lon", None),
        check_vma=False,
    )
```

time: 71 us -> 69.8 us (0.983)
  Pallas kernels: 5.12 us -> 4 us
where the time goes in v4:
time: 69.8 us; the launch traced here: 69.5 us
  blocking collectives  58.7 us (84%)
  starting transfers between devices  6.67 us (10%)
  Pallas kernels  4 us (6%)
    all_to_all x1, blocking collectives, per_device(): lax.all_to_all(packed.reshape(peers, cols, 1, depth), 'lon', 0, 0, axis_i...  32.5 us
    all_to_all x1, blocking collectives, per_device(): lax.all_to_all(filtered.reshape(peers, wide, 1, depth), 'lon', 0, 0, axis...  26.1 us
    ppermute x1, starting transfers between devices, per_device(): first = lax.ppermute(odd * tail + even * head, ('lat', 'lon'), first)  4.75 us
    ppermute x1, starting transfers between devices, per_device(): second = lax.ppermute(odd * head + even * tail, ('lat', 'lon'), second)  1.92 us
  transfers between devices with their start and end apart: 2, of which 0 were waited for; matrix products, arithmetic and copies ran while one was open for 0% of the time, Pallas kernels for 2%

profile of v4, /device:TPU:1, one launch (start us, length us, event | category | flops | bytes accessed | tf_op | source)
XLA Modules:
  0.0 69.5 jit_solution(6850985313944792749)
XLA Ops:
  0.0 0.0 copy-start
  0.0 0.0 copy-start.1
  0.0 0.0 copy-start.2
  0.0 1.2 %pack.1 = (f32[1152,128]{1,0:T(8,128)S(1)}, f32[1,1,128]{2,1,0:T(1,128)S(1)}, f32[1,1,128]{2,1,0:T(1,128)S(1)}) custom-call(f32[18,64,128]{2,1,0:T(8,128)} %bitcast.32), custom_call_target="tpu_custom_call" | custom-call | flops 10000000000 | bytes 67108864 | tf_op jit(solution)/shard_map/pack/pallas_call | solution.py:235
  1.2 32.5 %all_to_all.10 = f32[64,18,1,128]{3,2,1,0:T(1,128)S(1)} all-to-all(f32[64,18,1,128]{3,2,1,0:T(1,128)S(1)} %bitcast.26), channel_id=1, replica_groups={{0,1,2,3,4,5,6,7,8,9,10,11,12,13,14,15,31,30,29,28,27,26,25,24,23,22,21..., dimensions={0} | all-to-all | bytes 1179648 | tf_op jit(solution)/shard_map/all_to_all | solution.py:250
  33.8 0.0 copy-done
  33.8 0.0 copy-done.1
  33.8 0.0 copy-done.2
  33.8 0.0 copy-start.3
  33.8 0.0 copy-start.4
  33.8 0.0 copy-start.5
  33.8 0.9 %filter.1 = f32[1280,128]{1,0:T(8,128)S(1)} custom-call(s32[768]{0:T(1024)S(1)} %copy-done.1, s32[768]{0:T(1024)S(1)} %copy-done.2, f32[1152,128]{1,0:T(8,128)S(1)} %bitcast.24, bf16[1152,768]{1,0:T(8,128)(2,1)S(1)} %copy-done), custom_call_target="tpu_custom_call" | custom-call | tf_op jit(solution)/shard_map/filter/pallas_call | solution.py:252
  34.7 26.1 %all_to_all.11 = f32[64,20,1,128]{3,2,1,0:T(1,128)S(1)} all-to-all(f32[64,20,1,128]{3,2,1,0:T(1,128)S(1)} %bitcast.23), channel_id=1, replica_groups={{0,1,2,3,4,5,6,7,8,9,10,11,12,13,14,15,31,30,29,28,27,26,25,24,23,22,21..., dimensions={0} | all-to-all | bytes 1310720 | tf_op jit(solution)/shard_map/all_to_all | solution.py:266
  60.9 1.9 %collective-permute-start.1 = (f32[18,1,128]{2,1,0:T(1,128)S(1)}, f32[18,1,128]{2,1,0:T(1,128)S(1)}, u32[]{:S(2)}, u32[]{:S(2)}) collective-permute-start(f32[18,1,128]{2,1,0:T(1,128)S(1)} %get-tuple-element.19), channel_id=1, source_target_pairs={{0,64},{1,65},{2,66},{3,67},{4,68},{5,69},{6,70},{7,71},{8,72},{9,... | collective-permute-start | bytes 27656 | tf_op jit(solution)/shard_map/ppermute | solution.py:279
  62.8 4.7 %collective-permute-start = (f32[18,1,128]{2,1,0:T(1,128)S(1)}, f32[18,1,128]{2,1,0:T(1,128)S(1)}, u32[]{:S(2)}, u32[]{:S(2)}) collective-permute-start(f32[18,1,128]{2,1,0:T(1,128)S(1)} %get-tuple-element.20), channel_id=1, source_target_pairs={{0,32},{1,33},{2,34},{3,35},{4,36},{5,37},{6,38},{7,39},{8,40},{9,... | collective-permute-start | bytes 27656 | tf_op jit(solution)/shard_map/ppermute | solution.py:278
  67.6 0.0 copy-done.3
  67.6 0.0 copy-done.4
  67.6 0.0 copy-done.5
  67.6 1.1 %stencil.1 = (f32[18,64,128]{2,1,0:T(8,128)}, f32[2,18,8,128]{3,2,1,0:T(8,128)S(1)}, f32[2,18,1,128]{3,2,1,0:T(1,128)S(1)}, f32[12,48,128]{2,1,0:T(8,128)S(1)}) custom-call(f32[1280,128]{1,0:T(8,128)S(1)} %bitcast.25, f32[18,64]{1,0:T(8,128)S(1)} %bitcast.29, f32[18,64]{1,0:T(8,128)S(1)} %bitcast.30, f32[18,64]{1,0:T(8,128)S(1)} %bitcast.31), custom_call_target="tpu_custom_call" | custom-call | flops 1000000000 | bytes 2097152 | tf_op jit(solution)/shard_map/stencil/pallas_call | solution.py:281
  68.7 0.0 collective-permute-done.1.second_ref
  68.7 0.0 collective-permute-done.first_ref
  68.7 0.8 %rim.1 = f32[18,64,128]{2,1,0:T(8,128)} custom-call(f32[18,64,128]{2,1,0:T(8,128)} %get-tuple-element.13._, f32[2,18,8,128]{3,2,1,0:T(8,128)S(1)} %get-tuple-element.14.rim_ref, f32[2,18,1,128]{3,2,1,0:T(1,128)S(1)} %get-tuple-element.15.share_ref, f32[12,48,128]{2,1,0:T(8,128)S(1)} %get-tuple-element.16.late_ref, ...), custom_call_target="tpu_custom_call", output_to_operand_aliasing={{}: (0, {})} | custom-call | tf_op jit(solution)/shard_map/rim/pallas_call | solution.py:299
  (1 shorter events, 0.0 us)
Async XLA Ops:
  0.0 33.8 %copy-start = (bf16[1152,768]{1,0:T(8,128)(2,1)S(1)}, bf16[1152,768]{1,0:T(8,128)(2,1)}, u32[]{:S(2)}) copy-start(bf16[1152,768]{1,0:T(8,128)(2,1)} %constant.2.clone.table_ref) | copy-start | bytes 5308420
  0.0 33.8 %copy-start.1 = (s32[768]{0:T(1024)S(1)}, s32[768]{0:T(1024)}, u32[]{:S(2)}) copy-start(s32[768]{0:T(1024)} %cut_ref.1) | copy-start | bytes 9220
  0.0 33.8 %copy-start.2 = (s32[768]{0:T(1024)S(1)}, s32[768]{0:T(1024)}, u32[]{:S(2)}) copy-start(s32[768]{0:T(1024)} %cap_ref.1) | copy-start | bytes 9220
  33.8 33.8 %copy-start.3 = (f32[64,18]{0,1:T(8,128)S(1)}, f32[64,18]{0,1:T(8,128)}, u32[]{:S(2)}) copy-start(f32[64,18]{0,1:T(8,128)} %param.10) | copy-start | bytes 13828
  33.8 33.8 %copy-start.4 = (f32[64,18]{0,1:T(8,128)S(1)}, f32[64,18]{0,1:T(8,128)}, u32[]{:S(2)}) copy-start(f32[64,18]{0,1:T(8,128)} %param.11) | copy-start | bytes 13828
  33.8 33.8 %copy-start.5 = (f32[64,18]{0,1:T(8,128)S(1)}, f32[64,18]{0,1:T(8,128)}, u32[]{:S(2)}) copy-start(f32[64,18]{0,1:T(8,128)} %param.12) | copy-start | bytes 13828
  60.9 7.8 %collective-permute-start.1 = (f32[18,1,128]{2,1,0:T(1,128)S(1)}, f32[18,1,128]{2,1,0:T(1,128)S(1)}, u32[]{:S(2)}, u32[]{:S(2)}) collective-permute-start(f32[18,1,128]{2,1,0:T(1,128)S(1)} %get-tuple-element.19), channel_id=1, source_target_pairs={{0,64},{1,65},{2,66},{3,67},{4,68},{5,69},{6,70},{7,71},{8,72},{9,... | collective-permute-start | bytes 27656 | tf_op jit(solution)/shard_map/ppermute | solution.py:279
  62.8 5.9 %collective-permute-start = (f32[18,1,128]{2,1,0:T(1,128)S(1)}, f32[18,1,128]{2,1,0:T(1,128)S(1)}, u32[]{:S(2)}, u32[]{:S(2)}) collective-permute-start(f32[18,1,128]{2,1,0:T(1,128)S(1)} %get-tuple-element.20), channel_id=1, source_target_pairs={{0,32},{1,33},{2,34},{3,35},{4,36},{5,37},{6,38},{7,39},{8,40},{9,... | collective-permute-start | bytes 27656 | tf_op jit(solution)/shard_map/ppermute | solution.py:278

commit v5 on v4

--- a/solution.py
+++ b/solution.py
@@ -12,6 +12,7 @@
 LEV = 16
 WAVES = 288
 BACK_WIDTH = 384
+FIRST = 13
 STEPS = 1
 MIB = 1024 * 1024
 TILE = 8
@@ -27,7 +28,7 @@
 
 def ring(peers):
     count = peers // 4
-    return [q * count + (count - 1 - i if q % 2 else i) for q in range(4) for i in range(count)]
+    return [-q % 4 * count + (FIRST - i) % count for q in range(4) for i in range(count)]
 
 
 def pairs(cols):
@@ -35,12 +36,12 @@
 
 
 def tables(full, cols):
-    sectors = full // cols // 4
+    sectors = np.array(ring(full // cols)[: full // cols // 4])
     forth, back = [], []
     for parity in (0, 1):
         for curve in (np.cos, np.sin):
             for made, columns in ((forth, np.arange(cols)), (back, np.array(pairs(cols)))):
-                place = (columns[:, None] + cols * np.arange(sectors)[None, :]).reshape(-1)
+                place = (columns[:, None] + cols * sectors[None, :]).reshape(-1)
                 wave = np.arange(parity, WAVES, 2)
                 made.append(curve(wave[:, None] * (2 * place[None, :] + 1) % (2 * full) * (np.pi / full)))
     width = 2 * BACK_WIDTH
@@ -78,7 +79,7 @@
     return both[:, :depth] + both[:, depth:]
 
 
-def filter_kernel(cols, peers, cut_ref, cap_ref, x_ref, table_ref, out_ref, folds):
+def filter_kernel(cols, peers, cut_ref, cap_ref, x_ref, table_ref, out_ref, folds, turned, made_turned):
     depth = x_ref.shape[1]
     full = cols * peers
     count = peers // 4
@@ -86,43 +87,61 @@
     waves = WAVES // 2
     quarter = cols * count
     sector = lax.axis_index("lon")
-    turn = sector // count
-    place = jnp.where(turn % 2 == 1, (2 * turn + 1) * count - 1 - sector, sector)
-    row = lax.axis_index("lat") * peers + place
+    turn = (4 - sector // count) % 4
+    row = lax.axis_index("lat") * peers + turn * count + (FIRST + count - sector % count) % count
     line = lax.broadcasted_iota(jnp.int32, (1, cut_ref.shape[0]), 1)
     mine = jnp.where((line == row) & (cap_ref[...].reshape(line.shape) == 1), cut_ref[...].reshape(line.shape), 0)
     cut = jnp.max(mine.astype(jnp.float32)).astype(jnp.int32)
     index = lax.broadcasted_iota(jnp.int32, (count, depth), 0)
 
-    def lower(block, first):
-        return jnp.where(index == 0, first, pltpu.roll(block, 1, 0))
-
-    def upper(block, last):
-        return jnp.where(index == count - 1, last, pltpu.roll(block, count - 1, 0))
-
-    def emit(j, blocks):
-        a, b, c, d = blocks
-        rows = [(1 + j, blocks)]
-        if j == cols - 1:
-            rows.append((0, (lower(a, d[:1]), upper(b, a[-1:]), lower(c, b[:1]), upper(d, c[-1:]))))
-        if j == 0:
-            rows.append((wide - 1, (upper(a, b[-1:]), lower(b, c[:1]), upper(c, d[-1:]), lower(d, a[:1]))))
-        for i, values in rows:
-            out_ref[pl.ds(i, peers, stride=wide), :] = jnp.concatenate(values, axis=0)
-
-    def column(j):
-        return [x_ref[pl.ds(q * quarter + j, count, stride=cols), :] for q in range(4)]
+    last = {False: (FIRST + 1) % count, True: FIRST}
+    first = {False: FIRST, True: (FIRST + 1) % count}
+
+    def before(blocks, x, kinds):
+        other = (x - 1) % 4
+        edge = last[kinds[other]]
+        rolled = pltpu.roll(blocks[x], 1 if kinds[x] else count - 1, 0)
+        return jnp.where(index == first[kinds[x]], blocks[other][edge : edge + 1], rolled)
+
+    def after(blocks, x, kinds):
+        other = (x + 1) % 4
+        edge = first[kinds[other]]
+        rolled = pltpu.roll(blocks[x], count - 1 if kinds[x] else 1, 0)
+        return jnp.where(index == last[kinds[x]], blocks[other][edge : edge + 1], rolled)
+
+    def emit(j, blocks, kinds):
+        for x in range(4):
+            rows = [(1 + j, blocks[x])]
+            if j == cols - 1:
+                rows.append((0, before(blocks, x, kinds)))
+            if j == 0:
+                rows.append((wide - 1, after(blocks, x, kinds)))
+            for i, values in rows:
+                if kinds[x]:
+                    made_turned[x // 2, pl.ds(i, count, stride=wide), :] = values
+                else:
+                    out_ref[pl.ds(-x % 4 * count * wide + i, count, stride=wide), :] = values
+
+    def turn_over(i):
+        return (2 * FIRST + 1 - count - i) % count
+
+    def column(x, j):
+        return x_ref[pl.ds(-x % 4 * quarter + j, count, stride=cols), :]
 
     @pl.when(cut == 0)
     def _():
         for j in range(cols):
-            emit(j, column(j))
+            emit(j, [column(x, j) for x in range(4)], (False,) * 4)
 
     @pl.when(cut != 0)
     def _():
+        for x in (1, 3):
+            for i in range(count):
+                start = -x % 4 * quarter + turn_over(i) * cols
+                turned[x // 2, i * cols : (i + 1) * cols, :] = x_ref[start : start + cols, :]
         for j in range(cols):
-            a, _, c, _ = column(j)
-            _, b, _, d = column(cols - 1 - j)
+            a, c = column(0, j), column(2, j)
+            b, d = [turned[i, pl.ds(cols - 1 - j, count, stride=cols), :] for i in (0, 1)]
             for parity, (here, mirror) in enumerate(((a + c, d + b), (a - c, d - b))):
                 for kind, folded in enumerate((here + mirror, here - mirror)):
                     high, low = halves(folded)
@@ -152,7 +171,11 @@
                 made[j, 2], made[cols - 1 - j, 1] = (ce - co) + (se - so), (ce - co) - (se - so)
                 if t % 2 == 1:
                     for i in (order[k * step + t - 1], j):
-                        emit(i, [made[i, q] for q in range(4)])
+                        emit(i, [made[i, x] for x in range(4)], (False, True, False, True))
+        for x in (1, 3):
+            for i in range(count):
+                start = (-x % 4 * count + turn_over(i)) * wide
+                out_ref[start : start + wide, :] = made_turned[x // 2, i * wide : (i + 1) * wide, :]
 
 
 def stencil_kernel(cols, rows, n_lat, g_ref, cl_ref, ct_ref, cv_ref, out_ref, rim_ref, share_ref, late_ref, made, sems):
@@ -254,7 +277,11 @@
         out_shape=jax.ShapeDtypeStruct((peers * wide, depth), jnp.float32),
         in_specs=[vmem] * 4,
         out_specs=vmem,
-        scratch_shapes=[pltpu.VMEM((4, cols * peers // 4, 2 * depth), jnp.bfloat16)],
+        scratch_shapes=[
+            pltpu.VMEM((4, cols * peers // 4, 2 * depth), jnp.bfloat16),
+            pltpu.VMEM((2, cols * peers // 4, depth), jnp.float32),
+            pltpu.VMEM((2, wide * peers // 4, depth), jnp.float32),
+        ],
         compiler_params=pltpu.CompilerParams(vmem_limit_bytes=16 * MIB),
         name="filter",
     )(

time: 69.8 us -> 68.7 us (0.984)
  blocking collectives: 58.7 us -> 57.3 us
    all_to_all x1, blocking collectives: 26.1 us -> 25.2 us  [per_device(): lax.all_to_all(filtered.reshape(peers, wide, 1, depth), 'lon', 0, 0, axis...]
  transfers between devices with their start and end apart: 2 -> 2, of which waited for: 0 -> 1; matrix products, arithmetic and copies ran while one was open for 0% -> 0% of each run, Pallas kernels for 2% -> 2%
where the time goes in v5:
time: 68.7 us; the launch traced here: 68.2 us
  blocking collectives  57.3 us (83%)
  starting transfers between devices  6.02 us (9%)
  Pallas kernels  4.03 us (6%)
    all_to_all x1, blocking collectives, per_device(): lax.all_to_all(packed.reshape(peers, cols, 1, depth), 'lon', 0, 0, axis_i...  32.1 us
    all_to_all x1, blocking collectives, per_device(): lax.all_to_all(filtered.reshape(peers, wide, 1, depth), 'lon', 0, 0, axis...  25.2 us
    ppermute x1, starting transfers between devices, per_device(): first = lax.ppermute(odd * tail + even * head, ('lat', 'lon'), first)  4.1 us
    ppermute x1, starting transfers between devices, per_device(): second = lax.ppermute(odd * head + even * tail, ('lat', 'lon'), second)  1.92 us
  transfers between devices with their start and end apart: 2, of which 1 were waited for; matrix products, arithmetic and copies ran while one was open for 0% of the time, Pallas kernels for 2%

profile of v5, /device:TPU:1, one launch (start us, length us, event | category | flops | bytes accessed | tf_op | source)
XLA Modules:
  0.0 68.2 jit_solution(14539263910752108124)
XLA Ops:
  0.0 0.0 copy-start
  0.0 0.0 copy-start.1
  0.0 0.0 copy-start.2
  0.0 1.2 %pack.1 = (f32[1152,128]{1,0:T(8,128)S(1)}, f32[1,1,128]{2,1,0:T(1,128)S(1)}, f32[1,1,128]{2,1,0:T(1,128)S(1)}) custom-call(f32[18,64,128]{2,1,0:T(8,128)} %bitcast.32), custom_call_target="tpu_custom_call" | custom-call | flops 10000000000 | bytes 67108864 | tf_op jit(solution)/shard_map/pack/pallas_call | solution.py:258
  1.2 32.1 %all_to_all.10 = f32[64,18,1,128]{3,2,1,0:T(1,128)S(1)} all-to-all(f32[64,18,1,128]{3,2,1,0:T(1,128)S(1)} %bitcast.26), channel_id=1, replica_groups={{13,12,11,10,9,8,7,6,5,4,3,2,1,0,15,14,61,60,59,58,57,56,55,54,53,52,51..., dimensions={0} | all-to-all | bytes 1179648 | tf_op jit(solution)/shard_map/all_to_all | solution.py:273
  33.4 0.0 copy-done
  33.4 0.0 copy-done.1
  33.4 0.0 copy-done.2
  33.4 0.0 copy-start.3
  33.4 0.0 copy-start.4
  33.4 0.0 copy-start.5
  33.4 1.0 %filter.1 = f32[1280,128]{1,0:T(8,128)S(1)} custom-call(s32[768]{0:T(1024)S(1)} %copy-done.1, s32[768]{0:T(1024)S(1)} %copy-done.2, f32[1152,128]{1,0:T(8,128)S(1)} %bitcast.24, bf16[1152,768]{1,0:T(8,128)(2,1)S(1)} %copy-done), custom_call_target="tpu_custom_call" | custom-call | tf_op jit(solution)/shard_map/filter/pallas_call | solution.py:275
  34.4 25.2 %all_to_all.11 = f32[64,20,1,128]{3,2,1,0:T(1,128)S(1)} all-to-all(f32[64,20,1,128]{3,2,1,0:T(1,128)S(1)} %bitcast.23), channel_id=1, replica_groups={{13,12,11,10,9,8,7,6,5,4,3,2,1,0,15,14,61,60,59,58,57,56,55,54,53,52,51..., dimensions={0} | all-to-all | bytes 1310720 | tf_op jit(solution)/shard_map/all_to_all | solution.py:293
  59.6 1.9 %collective-permute-start.1 = (f32[18,1,128]{2,1,0:T(1,128)S(1)}, f32[18,1,128]{2,1,0:T(1,128)S(1)}, u32[]{:S(2)}, u32[]{:S(2)}) collective-permute-start(f32[18,1,128]{2,1,0:T(1,128)S(1)} %get-tuple-element.19), channel_id=1, source_target_pairs={{0,64},{1,65},{2,66},{3,67},{4,68},{5,69},{6,70},{7,71},{8,72},{9,... | collective-permute-start | bytes 27656 | tf_op jit(solution)/shard_map/ppermute | solution.py:306
  61.5 4.1 %collective-permute-start = (f32[18,1,128]{2,1,0:T(1,128)S(1)}, f32[18,1,128]{2,1,0:T(1,128)S(1)}, u32[]{:S(2)}, u32[]{:S(2)}) collective-permute-start(f32[18,1,128]{2,1,0:T(1,128)S(1)} %get-tuple-element.20), channel_id=1, source_target_pairs={{0,32},{1,33},{2,34},{3,35},{4,36},{5,37},{6,38},{7,39},{8,40},{9,... | collective-permute-start | bytes 27656 | tf_op jit(solution)/shard_map/ppermute | solution.py:305
  65.6 0.0 copy-done.3
  65.6 0.0 copy-done.4
  65.6 0.0 copy-done.5
  65.6 1.1 %stencil.1 = (f32[18,64,128]{2,1,0:T(8,128)}, f32[2,18,8,128]{3,2,1,0:T(8,128)S(1)}, f32[2,18,1,128]{3,2,1,0:T(1,128)S(1)}, f32[12,48,128]{2,1,0:T(8,128)S(1)}) custom-call(f32[1280,128]{1,0:T(8,128)S(1)} %bitcast.25, f32[18,64]{1,0:T(8,128)S(1)} %bitcast.29, f32[18,64]{1,0:T(8,128)S(1)} %bitcast.30, f32[18,64]{1,0:T(8,128)S(1)} %bitcast.31), custom_call_target="tpu_custom_call" | custom-call | flops 1000000000 | bytes 2097152 | tf_op jit(solution)/shard_map/stencil/pallas_call | solution.py:308
  66.7 0.0 collective-permute-done.1.second_ref
  66.7 0.7 collective-permute-done.first_ref
  67.4 0.8 %rim.1 = f32[18,64,128]{2,1,0:T(8,128)} custom-call(f32[18,64,128]{2,1,0:T(8,128)} %get-tuple-element.13._, f32[2,18,8,128]{3,2,1,0:T(8,128)S(1)} %get-tuple-element.14.rim_ref, f32[2,18,1,128]{3,2,1,0:T(1,128)S(1)} %get-tuple-element.15.share_ref, f32[12,48,128]{2,1,0:T(8,128)S(1)} %get-tuple-element.16.late_ref, ...), custom_call_target="tpu_custom_call", output_to_operand_aliasing={{}: (0, {})} | custom-call | tf_op jit(solution)/shard_map/rim/pallas_call | solution.py:326
  (1 shorter events, 0.0 us)
Async XLA Ops:
  0.0 33.4 %copy-start = (bf16[1152,768]{1,0:T(8,128)(2,1)S(1)}, bf16[1152,768]{1,0:T(8,128)(2,1)}, u32[]{:S(2)}) copy-start(bf16[1152,768]{1,0:T(8,128)(2,1)} %constant.2.clone.table_ref) | copy-start | bytes 5308420
  0.0 33.4 %copy-start.1 = (s32[768]{0:T(1024)S(1)}, s32[768]{0:T(1024)}, u32[]{:S(2)}) copy-start(s32[768]{0:T(1024)} %cut_ref.1) | copy-start | bytes 9220
  0.0 33.4 %copy-start.2 = (s32[768]{0:T(1024)S(1)}, s32[768]{0:T(1024)}, u32[]{:S(2)}) copy-start(s32[768]{0:T(1024)} %cap_ref.1) | copy-start | bytes 9220
  33.4 32.2 %copy-start.3 = (f32[64,18]{0,1:T(8,128)S(1)}, f32[64,18]{0,1:T(8,128)}, u32[]{:S(2)}) copy-start(f32[64,18]{0,1:T(8,128)} %param.10) | copy-start | bytes 13828
  33.4 32.2 %copy-start.4 = (f32[64,18]{0,1:T(8,128)S(1)}, f32[64,18]{0,1:T(8,128)}, u32[]{:S(2)}) copy-start(f32[64,18]{0,1:T(8,128)} %param.11) | copy-start | bytes 13828
  33.4 32.2 %copy-start.5 = (f32[64,18]{0,1:T(8,128)S(1)}, f32[64,18]{0,1:T(8,128)}, u32[]{:S(2)}) copy-start(f32[64,18]{0,1:T(8,128)} %param.12) | copy-start | bytes 13828
  59.6 7.2 %collective-permute-start.1 = (f32[18,1,128]{2,1,0:T(1,128)S(1)}, f32[18,1,128]{2,1,0:T(1,128)S(1)}, u32[]{:S(2)}, u32[]{:S(2)}) collective-permute-start(f32[18,1,128]{2,1,0:T(1,128)S(1)} %get-tuple-element.19), channel_id=1, source_target_pairs={{0,64},{1,65},{2,66},{3,67},{4,68},{5,69},{6,70},{7,71},{8,72},{9,... | collective-permute-start | bytes 27656 | tf_op jit(solution)/shard_map/ppermute | solution.py:306
  61.5 5.9 %collective-permute-start = (f32[18,1,128]{2,1,0:T(1,128)S(1)}, f32[18,1,128]{2,1,0:T(1,128)S(1)}, u32[]{:S(2)}, u32[]{:S(2)}) collective-permute-start(f32[18,1,128]{2,1,0:T(1,128)S(1)} %get-tuple-element.20), channel_id=1, source_target_pairs={{0,32},{1,33},{2,34},{3,35},{4,36},{5,37},{6,38},{7,39},{8,40},{9,... | collective-permute-start | bytes 27656 | tf_op jit(solution)/shard_map/ppermute | solution.py:305

commit v6 on v5

--- a/solution.py
+++ b/solution.py
@@ -12,7 +12,7 @@
 LEV = 16
 WAVES = 288
 BACK_WIDTH = 384
-FIRST = 13
+FIRST = 3
 STEPS = 1
 MIB = 1024 * 1024
 TILE = 8
@@ -28,7 +28,7 @@
 
 def ring(peers):
     count = peers // 4
-    return [-q % 4 * count + (FIRST - i) % count for q in range(4) for i in range(count)]
+    return [q % 4 * count + (FIRST - i) % count for q in range(4) for i in range(count)]
 
 
 def pairs(cols):
@@ -87,7 +87,7 @@
     waves = WAVES // 2
     quarter = cols * count
     sector = lax.axis_index("lon")
-    turn = (4 - sector // count) % 4
+    turn = sector // count
     row = lax.axis_index("lat") * peers + turn * count + (FIRST + count - sector % count) % count
     line = lax.broadcasted_iota(jnp.int32, (1, cut_ref.shape[0]), 1)
     mine = jnp.where((line == row) & (cap_ref[...].reshape(line.shape) == 1), cut_ref[...].reshape(line.shape), 0)
@@ -120,13 +120,13 @@
                 if kinds[x]:
                     made_turned[x // 2, pl.ds(i, count, stride=wide), :] = values
                 else:
-                    out_ref[pl.ds(-x % 4 * count * wide + i, count, stride=wide), :] = values
+                    out_ref[pl.ds(x % 4 * count * wide + i, count, stride=wide), :] = values
 
     def turn_over(i):
         return (2 * FIRST + 1 - count - i) % count
 
     def column(x, j):
-        return x_ref[pl.ds(-x % 4 * quarter + j, count, stride=cols), :]
+        return x_ref[pl.ds(x % 4 * quarter + j, count, stride=cols), :]
 
     @pl.when(cut == 0)
     def _():
@@ -137,7 +137,7 @@
     def _():
         for x in (1, 3):
             for i in range(count):
-                start = -x % 4 * quarter + turn_over(i) * cols
+                start = x % 4 * quarter + turn_over(i) * cols
                 turned[x // 2, i * cols : (i + 1) * cols, :] = x_ref[start : start + cols, :]
         for j in range(cols):
             a, c = column(0, j), column(2, j)
@@ -174,7 +174,7 @@
                         emit(i, [made[i, x] for x in range(4)], (False, True, False, True))
         for x in (1, 3):
             for i in range(count):
-                start = (-x % 4 * count + turn_over(i)) * wide
+                start = (x % 4 * count + turn_over(i)) * wide
                 out_ref[start : start + wide, :] = made_turned[x // 2, i * wide : (i + 1) * wide, :]
 
 

time: 68.7 us -> 68 us (0.990)
    all_to_all x1, blocking collectives: 32.1 us -> 31.1 us  [per_device(): lax.all_to_all(packed.reshape(peers, cols, 1, depth), 'lon', 0, 0, axis_i...]
where the time goes in v6:
time: 68 us; the launch traced here: 67.6 us
  blocking collectives  56.7 us (83%)
  starting transfers between devices  6.6 us (10%)
  Pallas kernels  4.03 us (6%)
    all_to_all x1, blocking collectives, per_device(): lax.all_to_all(packed.reshape(peers, cols, 1, depth), 'lon', 0, 0, axis_i...  31.1 us
    all_to_all x1, blocking collectives, per_device(): lax.all_to_all(filtered.reshape(peers, wide, 1, depth), 'lon', 0, 0, axis...  25.6 us
    ppermute x1, starting transfers between devices, per_device(): first = lax.ppermute(odd * tail + even * head, ('lat', 'lon'), first)  4.67 us
    ppermute x1, starting transfers between devices, per_device(): second = lax.ppermute(odd * head + even * tail, ('lat', 'lon'), second)  1.93 us
  transfers between devices with their start and end apart: 2, of which 1 were waited for; matrix products, arithmetic and copies ran while one was open for 0% of the time, Pallas kernels for 2%

profile of v6, /device:TPU:1, one launch (start us, length us, event | category | flops | bytes accessed | tf_op | source)
XLA Modules:
  0.0 67.6 jit_solution(4665135946522379918)
XLA Ops:
  0.0 0.0 copy-start
  0.0 0.0 copy-start.1
  0.0 0.0 copy-start.2
  0.0 1.2 %pack.1 = (f32[1152,128]{1,0:T(8,128)S(1)}, f32[1,1,128]{2,1,0:T(1,128)S(1)}, f32[1,1,128]{2,1,0:T(1,128)S(1)}) custom-call(f32[18,64,128]{2,1,0:T(8,128)} %bitcast.32), custom_call_target="tpu_custom_call" | custom-call | flops 10000000000 | bytes 67108864 | tf_op jit(solution)/shard_map/pack/pallas_call | solution.py:258
  1.2 31.1 %all_to_all.10 = f32[64,18,1,128]{3,2,1,0:T(1,128)S(1)} all-to-all(f32[64,18,1,128]{3,2,1,0:T(1,128)S(1)} %bitcast.26), channel_id=1, replica_groups={{3,2,1,0,15,14,13,12,11,10,9,8,7,6,5,4,19,18,17,16,31,30,29,28,27,26,25..., dimensions={0} | all-to-all | bytes 1179648 | tf_op jit(solution)/shard_map/all_to_all | solution.py:273
  32.4 0.0 copy-done
  32.4 0.0 copy-done.1
  32.4 0.0 copy-done.2
  32.4 0.0 copy-start.3
  32.4 0.0 copy-start.4
  32.4 0.0 copy-start.5
  32.4 1.0 %filter.1 = f32[1280,128]{1,0:T(8,128)S(1)} custom-call(s32[768]{0:T(1024)S(1)} %copy-done.1, s32[768]{0:T(1024)S(1)} %copy-done.2, f32[1152,128]{1,0:T(8,128)S(1)} %bitcast.24, bf16[1152,768]{1,0:T(8,128)(2,1)S(1)} %copy-done), custom_call_target="tpu_custom_call" | custom-call | tf_op jit(solution)/shard_map/filter/pallas_call | solution.py:275
  33.4 25.6 %all_to_all.11 = f32[64,20,1,128]{3,2,1,0:T(1,128)S(1)} all-to-all(f32[64,20,1,128]{3,2,1,0:T(1,128)S(1)} %bitcast.23), channel_id=1, replica_groups={{3,2,1,0,15,14,13,12,11,10,9,8,7,6,5,4,19,18,17,16,31,30,29,28,27,26,25..., dimensions={0} | all-to-all | bytes 1310720 | tf_op jit(solution)/shard_map/all_to_all | solution.py:293
  59.0 1.9 %collective-permute-start.1 = (f32[18,1,128]{2,1,0:T(1,128)S(1)}, f32[18,1,128]{2,1,0:T(1,128)S(1)}, u32[]{:S(2)}, u32[]{:S(2)}) collective-permute-start(f32[18,1,128]{2,1,0:T(1,128)S(1)} %get-tuple-element.19), channel_id=1, source_target_pairs={{0,64},{1,65},{2,66},{3,67},{4,68},{5,69},{6,70},{7,71},{8,72},{9,... | collective-permute-start | bytes 27656 | tf_op jit(solution)/shard_map/ppermute | solution.py:306
  60.9 4.7 %collective-permute-start = (f32[18,1,128]{2,1,0:T(1,128)S(1)}, f32[18,1,128]{2,1,0:T(1,128)S(1)}, u32[]{:S(2)}, u32[]{:S(2)}) collective-permute-start(f32[18,1,128]{2,1,0:T(1,128)S(1)} %get-tuple-element.20), channel_id=1, source_target_pairs={{0,32},{1,33},{2,34},{3,35},{4,36},{5,37},{6,38},{7,39},{8,40},{9,... | collective-permute-start | bytes 27656 | tf_op jit(solution)/shard_map/ppermute | solution.py:305
  65.6 0.0 copy-done.3
  65.6 0.0 copy-done.4
  65.6 0.0 copy-done.5
  65.6 1.1 %stencil.1 = (f32[18,64,128]{2,1,0:T(8,128)}, f32[2,18,8,128]{3,2,1,0:T(8,128)S(1)}, f32[2,18,1,128]{3,2,1,0:T(1,128)S(1)}, f32[12,48,128]{2,1,0:T(8,128)S(1)}) custom-call(f32[1280,128]{1,0:T(8,128)S(1)} %bitcast.25, f32[18,64]{1,0:T(8,128)S(1)} %bitcast.29, f32[18,64]{1,0:T(8,128)S(1)} %bitcast.30, f32[18,64]{1,0:T(8,128)S(1)} %bitcast.31), custom_call_target="tpu_custom_call" | custom-call | flops 1000000000 | bytes 2097152 | tf_op jit(solution)/shard_map/stencil/pallas_call | solution.py:308
  66.7 0.0 collective-permute-done.1.second_ref
  66.7 0.1 collective-permute-done.first_ref
  66.8 0.8 %rim.1 = f32[18,64,128]{2,1,0:T(8,128)} custom-call(f32[18,64,128]{2,1,0:T(8,128)} %get-tuple-element.13._, f32[2,18,8,128]{3,2,1,0:T(8,128)S(1)} %get-tuple-element.14.rim_ref, f32[2,18,1,128]{3,2,1,0:T(1,128)S(1)} %get-tuple-element.15.share_ref, f32[12,48,128]{2,1,0:T(8,128)S(1)} %get-tuple-element.16.late_ref, ...), custom_call_target="tpu_custom_call", output_to_operand_aliasing={{}: (0, {})} | custom-call | tf_op jit(solution)/shard_map/rim/pallas_call | solution.py:326
  (1 shorter events, 0.0 us)
Async XLA Ops:
  0.0 32.4 %copy-start = (bf16[1152,768]{1,0:T(8,128)(2,1)S(1)}, bf16[1152,768]{1,0:T(8,128)(2,1)}, u32[]{:S(2)}) copy-start(bf16[1152,768]{1,0:T(8,128)(2,1)} %constant.2.clone.table_ref) | copy-start | bytes 5308420
  0.0 32.4 %copy-start.1 = (s32[768]{0:T(1024)S(1)}, s32[768]{0:T(1024)}, u32[]{:S(2)}) copy-start(s32[768]{0:T(1024)} %cut_ref.1) | copy-start | bytes 9220
  0.0 32.4 %copy-start.2 = (s32[768]{0:T(1024)S(1)}, s32[768]{0:T(1024)}, u32[]{:S(2)}) copy-start(s32[768]{0:T(1024)} %cap_ref.1) | copy-start | bytes 9220
  32.4 33.2 %copy-start.3 = (f32[64,18]{0,1:T(8,128)S(1)}, f32[64,18]{0,1:T(8,128)}, u32[]{:S(2)}) copy-start(f32[64,18]{0,1:T(8,128)} %param.10) | copy-start | bytes 13828
  32.4 33.2 %copy-start.4 = (f32[64,18]{0,1:T(8,128)S(1)}, f32[64,18]{0,1:T(8,128)}, u32[]{:S(2)}) copy-start(f32[64,18]{0,1:T(8,128)} %param.11) | copy-start | bytes 13828
  32.4 33.2 %copy-start.5 = (f32[64,18]{0,1:T(8,128)S(1)}, f32[64,18]{0,1:T(8,128)}, u32[]{:S(2)}) copy-start(f32[64,18]{0,1:T(8,128)} %param.12) | copy-start | bytes 13828
  59.0 7.7 %collective-permute-start.1 = (f32[18,1,128]{2,1,0:T(1,128)S(1)}, f32[18,1,128]{2,1,0:T(1,128)S(1)}, u32[]{:S(2)}, u32[]{:S(2)}) collective-permute-start(f32[18,1,128]{2,1,0:T(1,128)S(1)} %get-tuple-element.19), channel_id=1, source_target_pairs={{0,64},{1,65},{2,66},{3,67},{4,68},{5,69},{6,70},{7,71},{8,72},{9,... | collective-permute-start | bytes 27656 | tf_op jit(solution)/shard_map/ppermute | solution.py:306
  60.9 5.9 %collective-permute-start = (f32[18,1,128]{2,1,0:T(1,128)S(1)}, f32[18,1,128]{2,1,0:T(1,128)S(1)}, u32[]{:S(2)}, u32[]{:S(2)}) collective-permute-start(f32[18,1,128]{2,1,0:T(1,128)S(1)} %get-tuple-element.20), channel_id=1, source_target_pairs={{0,32},{1,33},{2,34},{3,35},{4,36},{5,37},{6,38},{7,39},{8,40},{9,... | collective-permute-start | bytes 27656 | tf_op jit(solution)/shard_map/ppermute | solution.py:305

commit v7 on v6

--- a/solution.py
+++ b/solution.py
@@ -16,7 +16,7 @@
 STEPS = 1
 MIB = 1024 * 1024
 TILE = 8
-LATE = 12
+LATE = 9
 
 
 def pair_table(table, width):
@@ -28,7 +28,7 @@
 
 def ring(peers):
     count = peers // 4
-    return [q % 4 * count + (FIRST - i) % count for q in range(4) for i in range(count)]
+    return [q * count + (FIRST - i) % count for q in range(4) for i in range(count)]
 
 
 def pairs(cols):
@@ -120,13 +120,13 @@
                 if kinds[x]:
                     made_turned[x // 2, pl.ds(i, count, stride=wide), :] = values
                 else:
-                    out_ref[pl.ds(x % 4 * count * wide + i, count, stride=wide), :] = values
+                    out_ref[pl.ds(x * count * wide + i, count, stride=wide), :] = values
 
     def turn_over(i):
         return (2 * FIRST + 1 - count - i) % count
 
     def column(x, j):
-        return x_ref[pl.ds(x % 4 * quarter + j, count, stride=cols), :]
+        return x_ref[pl.ds(x * quarter + j, count, stride=cols), :]
 
     @pl.when(cut == 0)
     def _():
@@ -137,7 +137,7 @@
     def _():
         for x in (1, 3):
             for i in range(count):
-                start = x % 4 * quarter + turn_over(i) * cols
+                start = x * quarter + turn_over(i) * cols
                 turned[x // 2, i * cols : (i + 1) * cols, :] = x_ref[start : start + cols, :]
         for j in range(cols):
             a, c = column(0, j), column(2, j)
@@ -174,7 +174,7 @@
                         emit(i, [made[i, x] for x in range(4)], (False, True, False, True))
         for x in (1, 3):
             for i in range(count):
-                start = (x % 4 * count + turn_over(i)) * wide
+                start = (x * count + turn_over(i)) * wide
                 out_ref[start : start + wide, :] = made_turned[x // 2, i * wide : (i + 1) * wide, :]
 
 

time: 68 us -> 68 us (level)
  transfers between devices with their start and end apart: 2 -> 2, of which waited for: 1 -> 0; matrix products, arithmetic and copies ran while one was open for 0% -> 0% of each run, Pallas kernels for 2% -> 2%
where the time goes in v7:
time: 68 us; the launch traced here: 67.6 us
  blocking collectives  56.7 us (83%)
  starting transfers between devices  6.6 us (10%)
  Pallas kernels  4.17 us (6%)
    all_to_all x1, blocking collectives, per_device(): lax.all_to_all(packed.reshape(peers, cols, 1, depth), 'lon', 0, 0, axis_i...  31.1 us
    all_to_all x1, blocking collectives, per_device(): lax.all_to_all(filtered.reshape(peers, wide, 1, depth), 'lon', 0, 0, axis...  25.6 us
    ppermute x1, starting transfers between devices, per_device(): first = lax.ppermute(odd * tail + even * head, ('lat', 'lon'), first)  4.67 us
    ppermute x1, starting transfers between devices, per_device(): second = lax.ppermute(odd * head + even * tail, ('lat', 'lon'), second)  1.93 us
  transfers between devices with their start and end apart: 2, of which 0 were waited for; matrix products, arithmetic and copies ran while one was open for 0% of the time, Pallas kernels for 2%

profile of v7, /device:TPU:1, one launch (start us, length us, event | category | flops | bytes accessed | tf_op | source)
XLA Modules:
  0.0 67.6 jit_solution(13318920146061267865)
XLA Ops:
  0.0 0.0 copy-start
  0.0 0.0 copy-start.1
  0.0 0.0 copy-start.2
  0.0 1.2 %pack.1 = (f32[1152,128]{1,0:T(8,128)S(1)}, f32[1,1,128]{2,1,0:T(1,128)S(1)}, f32[1,1,128]{2,1,0:T(1,128)S(1)}) custom-call(f32[18,64,128]{2,1,0:T(8,128)} %bitcast.32), custom_call_target="tpu_custom_call" | custom-call | flops 10000000000 | bytes 67108864 | tf_op jit(solution)/shard_map/pack/pallas_call | solution.py:258
  1.2 31.1 %all_to_all.10 = f32[64,18,1,128]{3,2,1,0:T(1,128)S(1)} all-to-all(f32[64,18,1,128]{3,2,1,0:T(1,128)S(1)} %bitcast.26), channel_id=1, replica_groups={{3,2,1,0,15,14,13,12,11,10,9,8,7,6,5,4,19,18,17,16,31,30,29,28,27,26,25..., dimensions={0} | all-to-all | bytes 1179648 | tf_op jit(solution)/shard_map/all_to_all | solution.py:273
  32.4 0.0 copy-done
  32.4 0.0 copy-done.1
  32.4 0.0 copy-done.2
  32.4 0.0 copy-start.3
  32.4 0.0 copy-start.4
  32.4 0.0 copy-start.5
  32.4 1.0 %filter.1 = f32[1280,128]{1,0:T(8,128)S(1)} custom-call(s32[768]{0:T(1024)S(1)} %copy-done.1, s32[768]{0:T(1024)S(1)} %copy-done.2, f32[1152,128]{1,0:T(8,128)S(1)} %bitcast.24, bf16[1152,768]{1,0:T(8,128)(2,1)S(1)} %copy-done), custom_call_target="tpu_custom_call" | custom-call | tf_op jit(solution)/shard_map/filter/pallas_call | solution.py:275
  33.4 25.6 %all_to_all.11 = f32[64,20,1,128]{3,2,1,0:T(1,128)S(1)} all-to-all(f32[64,20,1,128]{3,2,1,0:T(1,128)S(1)} %bitcast.23), channel_id=1, replica_groups={{3,2,1,0,15,14,13,12,11,10,9,8,7,6,5,4,19,18,17,16,31,30,29,28,27,26,25..., dimensions={0} | all-to-all | bytes 1310720 | tf_op jit(solution)/shard_map/all_to_all | solution.py:293
  59.0 1.9 %collective-permute-start.1 = (f32[18,1,128]{2,1,0:T(1,128)S(1)}, f32[18,1,128]{2,1,0:T(1,128)S(1)}, u32[]{:S(2)}, u32[]{:S(2)}) collective-permute-start(f32[18,1,128]{2,1,0:T(1,128)S(1)} %get-tuple-element.19), channel_id=1, source_target_pairs={{0,64},{1,65},{2,66},{3,67},{4,68},{5,69},{6,70},{7,71},{8,72},{9,... | collective-permute-start | bytes 27656 | tf_op jit(solution)/shard_map/ppermute | solution.py:306
  60.9 4.7 %collective-permute-start = (f32[18,1,128]{2,1,0:T(1,128)S(1)}, f32[18,1,128]{2,1,0:T(1,128)S(1)}, u32[]{:S(2)}, u32[]{:S(2)}) collective-permute-start(f32[18,1,128]{2,1,0:T(1,128)S(1)} %get-tuple-element.20), channel_id=1, source_target_pairs={{0,32},{1,33},{2,34},{3,35},{4,36},{5,37},{6,38},{7,39},{8,40},{9,... | collective-permute-start | bytes 27656 | tf_op jit(solution)/shard_map/ppermute | solution.py:305
  65.6 0.0 copy-done.3
  65.6 0.0 copy-done.4
  65.6 0.0 copy-done.5
  65.6 1.2 %stencil.1 = (f32[18,64,128]{2,1,0:T(8,128)}, f32[2,18,8,128]{3,2,1,0:T(8,128)S(1)}, f32[2,18,1,128]{3,2,1,0:T(1,128)S(1)}, f32[9,48,128]{2,1,0:T(8,128)S(1)}) custom-call(f32[1280,128]{1,0:T(8,128)S(1)} %bitcast.25, f32[18,64]{1,0:T(8,128)S(1)} %bitcast.29, f32[18,64]{1,0:T(8,128)S(1)} %bitcast.30, f32[18,64]{1,0:T(8,128)S(1)} %bitcast.31), custom_call_target="tpu_custom_call" | custom-call | flops 1000000000 | bytes 2097152 | tf_op jit(solution)/shard_map/stencil/pallas_call | solution.py:308
  66.8 0.0 collective-permute-done.1.second_ref
  66.9 0.0 collective-permute-done.first_ref
  66.9 0.8 %rim.1 = f32[18,64,128]{2,1,0:T(8,128)} custom-call(f32[18,64,128]{2,1,0:T(8,128)} %get-tuple-element.13._, f32[2,18,8,128]{3,2,1,0:T(8,128)S(1)} %get-tuple-element.14.rim_ref, f32[2,18,1,128]{3,2,1,0:T(1,128)S(1)} %get-tuple-element.15.share_ref, f32[9,48,128]{2,1,0:T(8,128)S(1)} %get-tuple-element.16.late_ref, ...), custom_call_target="tpu_custom_call", output_to_operand_aliasing={{}: (0, {})} | custom-call | tf_op jit(solution)/shard_map/rim/pallas_call | solution.py:326
  (1 shorter events, 0.0 us)
Async XLA Ops:
  0.0 32.4 %copy-start = (bf16[1152,768]{1,0:T(8,128)(2,1)S(1)}, bf16[1152,768]{1,0:T(8,128)(2,1)}, u32[]{:S(2)}) copy-start(bf16[1152,768]{1,0:T(8,128)(2,1)} %constant.2.clone.table_ref) | copy-start | bytes 5308420
  0.0 32.4 %copy-start.1 = (s32[768]{0:T(1024)S(1)}, s32[768]{0:T(1024)}, u32[]{:S(2)}) copy-start(s32[768]{0:T(1024)} %cut_ref.1) | copy-start | bytes 9220
  0.0 32.4 %copy-start.2 = (s32[768]{0:T(1024)S(1)}, s32[768]{0:T(1024)}, u32[]{:S(2)}) copy-start(s32[768]{0:T(1024)} %cap_ref.1) | copy-start | bytes 9220
  32.4 33.2 %copy-start.3 = (f32[64,18]{0,1:T(8,128)S(1)}, f32[64,18]{0,1:T(8,128)}, u32[]{:S(2)}) copy-start(f32[64,18]{0,1:T(8,128)} %param.10) | copy-start | bytes 13828
  32.4 33.2 %copy-start.4 = (f32[64,18]{0,1:T(8,128)S(1)}, f32[64,18]{0,1:T(8,128)}, u32[]{:S(2)}) copy-start(f32[64,18]{0,1:T(8,128)} %param.11) | copy-start | bytes 13828
  32.4 33.2 %copy-start.5 = (f32[64,18]{0,1:T(8,128)S(1)}, f32[64,18]{0,1:T(8,128)}, u32[]{:S(2)}) copy-start(f32[64,18]{0,1:T(8,128)} %param.12) | copy-start | bytes 13828
  59.0 7.9 %collective-permute-start.1 = (f32[18,1,128]{2,1,0:T(1,128)S(1)}, f32[18,1,128]{2,1,0:T(1,128)S(1)}, u32[]{:S(2)}, u32[]{:S(2)}) collective-permute-start(f32[18,1,128]{2,1,0:T(1,128)S(1)} %get-tuple-element.19), channel_id=1, source_target_pairs={{0,64},{1,65},{2,66},{3,67},{4,68},{5,69},{6,70},{7,71},{8,72},{9,... | collective-permute-start | bytes 27656 | tf_op jit(solution)/shard_map/ppermute | solution.py:306
  60.9 6.0 %collective-permute-start = (f32[18,1,128]{2,1,0:T(1,128)S(1)}, f32[18,1,128]{2,1,0:T(1,128)S(1)}, u32[]{:S(2)}, u32[]{:S(2)}) collective-permute-start(f32[18,1,128]{2,1,0:T(1,128)S(1)} %get-tuple-element.20), channel_id=1, source_target_pairs={{0,32},{1,33},{2,34},{3,35},{4,36},{5,37},{6,38},{7,39},{8,40},{9,... | collective-permute-start | bytes 27656 | tf_op jit(solution)/shard_map/ppermute | solution.py:305
